TPU v7x, 32 devices: a whole 2x2x4 slice. The times are simulated.
32 devices in a mesh: rep: 8 (over z, x), shard: 4 (over y, core).
Axes of the slice: x: 2, y: 2, z: 4, core: 2. Of those that a mesh axis runs over, the one named last changes fastest.
Arguments:
- hidden_in: bfloat16 [32768, 768], P(('rep', 'shard')), may hold values from -6 to 6
- segment_ids: int32 [32768], P(('rep', 'shard')), may hold values from -1 to 127, as said below
- cotangent: bfloat16 [32768, 768], P(('rep', 'shard')), may hold values from -6 to 6
- ln1_gain: bfloat16 [768], P('shard'), may hold values from 0.5 to 1.5
- ln1_bias: bfloat16 [768], P('shard'), may hold values from -1.5 to 1.5
- ln2_gain: bfloat16 [768], P('shard'), may hold values from 0.5 to 1.5
- ln2_bias: bfloat16 [768], P('shard'), may hold values from -1.5 to 1.5
- qkv_weight: bfloat16 [768, 2304], P('shard'), may hold values from -0.21875 to 0.21875
- qkv_bias: bfloat16 [2304], P('shard'), may hold values from -1.5 to 1.5
- out_weight: bfloat16 [768, 768], P('shard'), may hold values from -0.875 to 0.875
- out_bias: bfloat16 [768], P('shard'), may hold values from -1.5 to 1.5
- up_weight: bfloat16 [768, 3072], P('shard'), may hold values from -0.21875 to 0.21875
- up_bias: bfloat16 [3072], P('shard'), may hold values from -2.5 to 2.5
- down_weight: bfloat16 [3072, 768], P('shard'), may hold values from -0.109375 to 0.109375
- down_bias: bfloat16 [768], P('shard'), may hold values from -1.5 to 1.5
Outputs:
- mixed: bfloat16 [32768, 768], P(('rep', 'shard'))
- input_grad: float32 [32768, 768], P(('rep', 'shard'))
- grad_ln1_gain: float32 [768], P('shard')
- grad_ln1_bias: float32 [768], P('shard')
- grad_ln2_gain: float32 [768], P('shard')
- grad_ln2_bias: float32 [768], P('shard')
- grad_qkv_weight: float32 [768, 2304], P('shard')
- grad_qkv_bias: float32 [2304], P('shard')
- grad_out_weight: float32 [768, 768], P('shard')
- grad_out_bias: float32 [768], P('shard')
- grad_up_weight: float32 [768, 3072], P('shard')
- grad_up_bias: float32 [3072], P('shard')
- grad_down_weight: float32 [3072, 768], P('shard')
- grad_down_bias: float32 [768], P('shard')
Inputs may be any that keep to these rules, and one draw needn't show every extreme that they name: `segment_ids`: A sequence is a run of slots with one id 0 or more; its slots are consecutive, lie within one device's 1024 slots and number at most 1024; ids differ between sequences and rise along the slots; -1 marks unused slots, which come after a device's sequences; every device uses at least half of its slots, and some device holds a sequence of exactly 1024 slots.
All inputs are finite; a program needn't handle non-finite values.
Results may differ from a plain program's by a relative error of at most 0.0093.
Values may be sent and summed in bfloat16 or wider, within the bound.
A program may use at most 192 MiB of HBM per device.

v0:
```python
import jax
import jax.numpy as jnp
from jax import lax
from jax.sharding import PartitionSpec as P

D = 768
HEADS = 12
HEAD_DIM = 64
ROTARY = 16


EPS = 1e-05


def layer_norm(values, gain, bias):
    center = values - jnp.mean(values, -1, keepdims=True)
    spread = jnp.mean(center * center, -1, keepdims=True)
    return center * lax.rsqrt(spread + EPS) * gain + bias


def exact_gelu(values):
    return jax.nn.gelu(values, approximate=False)


def positions(segments):
    slot_index = jnp.arange(segments.shape[0], dtype=jnp.int32)
    is_start = jnp.concatenate([jnp.ones((1,), bool), segments[1:] != segments[:-1]])
    seq_start = lax.cummax(jnp.where(is_start, slot_index, jnp.zeros_like(slot_index)), axis=0)
    return slot_index - seq_start


def angles(places):
    rates = 10000.0 ** (-(jnp.arange(ROTARY // 2, dtype=jnp.float32) * 2.0) / ROTARY)
    turned = places.astype(jnp.float32)[:, None] * rates[None, :]
    turned = jnp.concatenate([turned, turned], -1)
    return (jnp.cos(turned)[:, None, :], jnp.sin(turned)[:, None, :])


def rotate(heads_in, cosine, sine_table):
    front = heads_in[..., :ROTARY]
    half = ROTARY // 2
    swapped = jnp.concatenate([-front[..., half:], front[..., :half]], -1)
    return jnp.concatenate([front * cosine + swapped * sine_table, heads_in[..., ROTARY:]], -1)


def place_heads(qkv, cosine, sine_table):
    length = qkv.shape[0]
    split = qkv.reshape(length, 3, HEADS, HEAD_DIM)
    query_rows = rotate(split[:, 0], cosine, sine_table).reshape(length, D)
    key_rows = rotate(split[:, 1], cosine, sine_table).reshape(length, D)
    return (query_rows, key_rows, split[:, 2].reshape(length, D))


def contract_rows(left, right):
    return lax.dot_general(
        left, right, (((0,), (0,)), ((), ())), preferred_element_type=jnp.float32
    )


def across(left, right):
    return lax.dot_general(
        left, right, (((1,), (1,)), ((), ())), preferred_element_type=jnp.float32
    )


def to_pairs(values):
    return values.reshape(values.shape[0], HEADS // 2, 2 * HEAD_DIM).transpose(1, 0, 2)


def from_pairs(values):
    return values.transpose(1, 0, 2).reshape(values.shape[1], D)


def block_mask(segments, first_row, block_rows):
    length = segments.shape[0]
    block_seg = lax.dynamic_slice_in_dim(segments, first_row, block_rows, 0)
    rows_here = first_row + jnp.arange(block_rows)
    return (block_seg[:, None] == segments[None, :]) & (
        rows_here[:, None] >= jnp.arange(length)[None, :]
    )


def attend(query_rows, key_rows, value_rows, segments):
    length = segments.shape[0]
    block_rows = min(512, length)
    block_count = length // block_rows

    def one_pair(trio):
        query_h, key_h, value_h = tuple((item.reshape(length, 2, HEAD_DIM) for item in trio))

        def one_block(number):
            first_row = number * block_rows
            query_block = lax.dynamic_slice_in_dim(query_h, first_row, block_rows, 0)
            readable = block_mask(segments, first_row, block_rows)
            scores = (
                jnp.einsum("qhd,khd->hqk", query_block, key_h, preferred_element_type=jnp.float32)
                * 0.125
            )
            scores = jnp.where(readable[None], scores, -1e30)
            highest = jnp.max(scores, -1, keepdims=True)
            raised = jnp.exp(scores - highest)
            summed = jnp.sum(raised, -1, keepdims=True)
            weights = (raised / summed).astype(jnp.bfloat16)
            result = jnp.einsum(
                "hqk,khd->qhd", weights, value_h, preferred_element_type=jnp.float32
            )
            return (
                result.astype(jnp.bfloat16).reshape(block_rows, 2 * HEAD_DIM),
                (highest + jnp.log(summed))[..., 0],
            )

        outs, log_total = lax.map(one_block, jnp.arange(block_count))
        return (outs.reshape(length, 2 * HEAD_DIM), log_total)

    outs, log_total = lax.map(
        one_pair, (to_pairs(query_rows), to_pairs(key_rows), to_pairs(value_rows))
    )
    return (from_pairs(outs), log_total)


def attend_back(query_rows, key_rows, value_rows, grad_out, log_total, segments):
    length = segments.shape[0]
    block_rows = min(512, length)
    block_count = length // block_rows

    def one_pair(items):
        query_h, key_h, value_h, grad_h = tuple(
            (item.reshape(length, 2, HEAD_DIM) for item in items[:4])
        )
        pair_total = items[4]
        empty = jnp.zeros((length, 2, HEAD_DIM), jnp.float32)

        def advance(running, number):
            grad_keys, grad_values = running
            first_row = number * block_rows
            query_block = lax.dynamic_slice_in_dim(query_h, first_row, block_rows, 0)
            grad_block = lax.dynamic_slice_in_dim(grad_h, first_row, block_rows, 0)
            readable = block_mask(segments, first_row, block_rows)
            scores = (
                jnp.einsum("qhd,khd->hqk", query_block, key_h, preferred_element_type=jnp.float32)
                * 0.125
            )
            weights = jnp.where(
                readable[None], jnp.exp(scores - pair_total[number][..., None]), 0.0
            )
            weights_low = weights.astype(jnp.bfloat16)
            grad_values = grad_values + jnp.einsum(
                "hqk,qhd->khd", weights_low, grad_block, preferred_element_type=jnp.float32
            )
            grad_weights = jnp.einsum(
                "qhd,khd->hqk", grad_block, value_h, preferred_element_type=jnp.float32
            )
            centre_term = jnp.sum(weights * grad_weights, -1, keepdims=True)
            grad_scores = (weights * (grad_weights - centre_term)).astype(jnp.bfloat16)
            grad_query = (
                jnp.einsum("hqk,khd->qhd", grad_scores, key_h, preferred_element_type=jnp.float32)
                * 0.125
            )
            grad_keys = (
                grad_keys
                + jnp.einsum(
                    "hqk,qhd->khd", grad_scores, query_block, preferred_element_type=jnp.float32
                )
                * 0.125
            )
            return ((grad_keys, grad_values), grad_query.reshape(block_rows, 2 * HEAD_DIM))

        (grad_keys, grad_values), grad_query = lax.scan(
            advance, (empty, empty), jnp.arange(block_count)
        )
        return (
            grad_query.reshape(length, 2 * HEAD_DIM),
            grad_keys.reshape(length, 2 * HEAD_DIM),
            grad_values.reshape(length, 2 * HEAD_DIM),
        )

    grad_query, grad_keys, grad_values = lax.map(
        one_pair,
        (
            to_pairs(query_rows),
            to_pairs(key_rows),
            to_pairs(value_rows),
            to_pairs(grad_out),
            log_total,
        ),
    )
    return (from_pairs(grad_query), from_pairs(grad_keys), from_pairs(grad_values))


def local(
    hidden_in,
    segment_ids,
    cotangent,
    ln1_gain,
    ln1_bias,
    ln2_gain,
    ln2_bias,
    qkv_weight,
    qkv_bias,
    out_weight,
    out_bias,
    up_weight,
    up_bias,
    down_weight,
    down_bias,
):
    gathered = (
        lax.all_gather(ln1_gain, "shard", axis=0, tiled=True),
        lax.all_gather(ln1_bias, "shard", axis=0, tiled=True),
        lax.all_gather(ln2_gain, "shard", axis=0, tiled=True),
        lax.all_gather(ln2_bias, "shard", axis=0, tiled=True),
        lax.all_gather(qkv_weight, "shard", axis=0, tiled=True),
        lax.all_gather(qkv_bias, "shard", axis=0, tiled=True),
        lax.all_gather(out_weight, "shard", axis=0, tiled=True),
        lax.all_gather(out_bias, "shard", axis=0, tiled=True),
        lax.all_gather(up_weight, "shard", axis=0, tiled=True),
        lax.all_gather(up_bias, "shard", axis=0, tiled=True),
        lax.all_gather(down_weight, "shard", axis=0, tiled=True),
        lax.all_gather(down_bias, "shard", axis=0, tiled=True),
    )
    w_qkv = gathered[4]
    w_out = gathered[6]
    w_up = gathered[8]
    w_down = gathered[10]
    gain_one, bias_one, gain_two, bias_two = tuple(
        (item.astype(jnp.float32) for item in gathered[:4])
    )
    b_qkv = gathered[5].astype(jnp.float32)
    b_out = gathered[7].astype(jnp.float32)
    b_up = gathered[9].astype(jnp.float32)
    b_down = gathered[11].astype(jnp.float32)
    x_float = hidden_in.astype(jnp.float32)
    cosine, sine_table = angles(positions(segment_ids))
    first_norm, norm_one_back = jax.vjp(layer_norm, x_float, gain_one, bias_one)
    first_in = first_norm.astype(jnp.bfloat16)
    qkv = jnp.dot(first_in, w_qkv, preferred_element_type=jnp.float32) + b_qkv
    (query_f, key_f, value_f), unplace = jax.vjp(
        lambda inner_qkv: place_heads(inner_qkv, cosine, sine_table), qkv
    )
    query_rows = query_f.astype(jnp.bfloat16)
    key_rows = key_f.astype(jnp.bfloat16)
    value_rows = value_f.astype(jnp.bfloat16)
    attended, log_total = attend(query_rows, key_rows, value_rows, segment_ids)
    attn = jnp.dot(attended, w_out, preferred_element_type=jnp.float32) + b_out
    second_norm, norm_two_back = jax.vjp(layer_norm, x_float, gain_two, bias_two)
    second_in = second_norm.astype(jnp.bfloat16)
    upward = jnp.dot(second_in, w_up, preferred_element_type=jnp.float32) + b_up
    active, gelu_back = jax.vjp(exact_gelu, upward)
    active_low = active.astype(jnp.bfloat16)
    feed = jnp.dot(active_low, w_down, preferred_element_type=jnp.float32) + b_down
    mixed = (x_float + attn + feed).astype(jnp.bfloat16)
    regathered = (
        lax.all_gather(ln1_gain, "shard", axis=0, tiled=True),
        lax.all_gather(ln1_bias, "shard", axis=0, tiled=True),
        lax.all_gather(ln2_gain, "shard", axis=0, tiled=True),
        lax.all_gather(ln2_bias, "shard", axis=0, tiled=True),
        lax.all_gather(qkv_weight, "shard", axis=0, tiled=True),
        lax.all_gather(qkv_bias, "shard", axis=0, tiled=True),
        lax.all_gather(out_weight, "shard", axis=0, tiled=True),
        lax.all_gather(out_bias, "shard", axis=0, tiled=True),
        lax.all_gather(up_weight, "shard", axis=0, tiled=True),
        lax.all_gather(up_bias, "shard", axis=0, tiled=True),
        lax.all_gather(down_weight, "shard", axis=0, tiled=True),
        lax.all_gather(down_bias, "shard", axis=0, tiled=True),
    )
    w_qkv = regathered[4]
    w_out = regathered[6]
    w_up = regathered[8]
    w_down = regathered[10]
    valid = (segment_ids >= 0)[:, None]
    grad_y = jnp.where(valid, cotangent, jnp.zeros_like(cotangent))
    grad_y_float = grad_y.astype(jnp.float32)
    grad_down = contract_rows(active_low, grad_y)
    grad_bias_y = jnp.sum(grad_y_float, 0)
    grad_active = across(grad_y, w_down)
    grad_upward = gelu_back(grad_active)[0].astype(jnp.bfloat16)
    grad_up = contract_rows(second_in, grad_upward)
    grad_up_bias = jnp.sum(grad_upward.astype(jnp.float32), 0)
    grad_second = across(grad_upward, w_up)
    grad_x_two, grad_gain_two, grad_bias_two = norm_two_back(grad_second)
    grad_out = contract_rows(attended, grad_y)
    grad_attended = across(grad_y, w_out).astype(jnp.bfloat16)
    grad_query, grad_keys, grad_values = attend_back(
        query_rows, key_rows, value_rows, grad_attended, log_total, segment_ids
    )
    grad_qkv = unplace((grad_query, grad_keys, grad_values))[0].astype(jnp.bfloat16)
    grad_qkv_w = contract_rows(first_in, grad_qkv)
    grad_qkv_b = jnp.sum(grad_qkv.astype(jnp.float32), 0)
    grad_first = across(grad_qkv, w_qkv)
    grad_x_one, grad_gain_one, grad_bias_one = norm_one_back(grad_first)
    input_grad = grad_y_float + grad_x_one + grad_x_two
    shares = (
        lax.psum_scatter(grad_gain_one, "shard", scatter_dimension=0, tiled=True),
        lax.psum_scatter(grad_bias_one, "shard", scatter_dimension=0, tiled=True),
        lax.psum_scatter(grad_gain_two, "shard", scatter_dimension=0, tiled=True),
        lax.psum_scatter(grad_bias_two, "shard", scatter_dimension=0, tiled=True),
        lax.psum_scatter(grad_qkv_w, "shard", scatter_dimension=0, tiled=True),
        lax.psum_scatter(grad_qkv_b, "shard", scatter_dimension=0, tiled=True),
        lax.psum_scatter(grad_out, "shard", scatter_dimension=0, tiled=True),
        lax.psum_scatter(grad_bias_y, "shard", scatter_dimension=0, tiled=True),
        lax.psum_scatter(grad_up, "shard", scatter_dimension=0, tiled=True),
        lax.psum_scatter(grad_up_bias, "shard", scatter_dimension=0, tiled=True),
        lax.psum_scatter(grad_down, "shard", scatter_dimension=0, tiled=True),
        lax.psum_scatter(grad_bias_y, "shard", scatter_dimension=0, tiled=True),
    )
    totals = lax.psum(
        (
            shares[0],
            shares[1],
            shares[2],
            shares[3],
            shares[4],
            shares[5],
            shares[6],
            shares[7],
            shares[8],
            shares[9],
            shares[10],
            shares[11],
        ),
        "rep",
    )
    return (
        mixed,
        input_grad,
        totals[0],
        totals[1],
        totals[2],
        totals[3],
        totals[4],
        totals[5],
        totals[6],
        totals[7],
        totals[8],
        totals[9],
        totals[10],
        totals[11],
    )


def solution(mesh):
    return jax.shard_map(
        local,
        mesh=mesh,
        in_specs=(
            P(("rep", "shard"), None),
            P(("rep", "shard")),
            P(("rep", "shard"), None),
            P("shard"),
            P("shard"),
            P("shard"),
            P("shard"),
            P("shard", None),
            P("shard"),
            P("shard", None),
            P("shard"),
            P("shard", None),
            P("shard"),
            P("shard", None),
            P("shard"),
        ),
        out_specs=(
            P(("rep", "shard"), None),
            P(("rep", "shard"), None),
            P("shard"),
            P("shard"),
            P("shard"),
            P("shard"),
            P("shard", None),
            P("shard"),
            P("shard", None),
            P("shard"),
            P("shard", None),
            P("shard"),
            P("shard", None),
            P("shard"),
        ),
        check_vma=False,
    )
```

profile of v0, /device:TPU:0, one launch (start us, length us, event | category | flops | bytes accessed | tf_op | source)
XLA Modules:
  0.0 981.2 jit_solution(15101667248762249191)
XLA Ops:
  13.9 14.6 %all-reduce.28 = (bf16[768]{0:T(1024)(128)(2,1)}, bf16[768]{0:T(1024)(128)(2,1)}, bf16[2304]{0:T(1024)(128)(2,1)S(1)}, bf16[768]{0:T(1024)(128)(2,1)S(1)}, bf16[...) all-reduce(bf16[768]{0:T(1024)(128)(2,1)S(1)} %dynamic-update-slice, ...), channel_id=1, replica_groups=mesh['rep'=8,'shard'=4] {'shard'}, use_global_device_ids=true, to_apply=%add.16 | all-reduce | flops 6912 | bytes 27648
  34.4 28.2 %all-gather.6.cloned.1.call-done = bf16[768,2304]{1,0:T(8,128)(2,1)} async-done(((bf16[192,2304]{1,0:T(8,128)(2,1)}), bf16[768,2304]{1,0:T(8,128)(2,1)}) %all-gather.6.cloned.1.call-update) | async-done | bytes 3538960 | tf_op jit(solution)/shard_map/all_gather | solution.py:212
  62.6 8.7 convolution_add_fusion
  71.3 9.8 %copy.49 = f32[1024,2304]{0,1:T(8,128)} copy(f32[1024,2304]{1,0:T(8,128)} %convolution_add_fusion) | data formatting | bytes 18874368 | tf_op jit(solution)/shard_map/add | solution.py:236
  90.2 87.6 %while.54 = (s32[]{:T(128)}, bf16[6,1024,128]{1,2,0:T(8,128)(2,1)}, f32[6,2,2,512]{3,2,1,0:T(2,128)S(1)}, bf16[6,1024,128]{1,2,0:T(8,128)(2,1)}, bf16[6,1024,128...) while((s32[]{:T(128)}, bf16[6,1024,128]{1,2,0:T(8,128)(2,1)}, ...), condition=%wide.region_9.10_spmd, body=%wide.region_4.9_spmd.sunk | while | flops 282656256 | bytes 18676676 | solution.py:115
  92.2 11.7 %while.57 = (s32[]{:T(128)}, bf16[2,512,128]{2,1,0:T(8,128)(2,1)S(1)}, f32[2,2,512]{2,1,0:T(2,128)S(1)}, s32[2]{0:T(128)S(1)}, s32[1024]{0:T(1024)S(1)}, /*index...) while((s32[]{:T(128)}, ...), condition=%wide.region_8.8_spmd, body=%wide.region_5.7_spmd.sunk | while | flops 282656256 | bytes 16038083 | solution.py:112
  106.8 11.7 %while.57 = (s32[]{:T(128)}, bf16[2,512,128]{2,1,0:T(8,128)(2,1)S(1)}, f32[2,2,512]{2,1,0:T(2,128)S(1)}, s32[2]{0:T(128)S(1)}, s32[1024]{0:T(1024)S(1)}, /*index...) while((s32[]{:T(128)}, ...), condition=%wide.region_8.8_spmd, body=%wide.region_5.7_spmd.sunk | while | flops 282656256 | bytes 16038083 | solution.py:112
  121.3 11.7 %while.57 = (s32[]{:T(128)}, bf16[2,512,128]{2,1,0:T(8,128)(2,1)S(1)}, f32[2,2,512]{2,1,0:T(2,128)S(1)}, s32[2]{0:T(128)S(1)}, s32[1024]{0:T(1024)S(1)}, /*index...) while((s32[]{:T(128)}, ...), condition=%wide.region_8.8_spmd, body=%wide.region_5.7_spmd.sunk | while | flops 282656256 | bytes 16038083 | solution.py:112
  135.9 11.7 %while.57 = (s32[]{:T(128)}, bf16[2,512,128]{2,1,0:T(8,128)(2,1)S(1)}, f32[2,2,512]{2,1,0:T(2,128)S(1)}, s32[2]{0:T(128)S(1)}, s32[1024]{0:T(1024)S(1)}, /*index...) while((s32[]{:T(128)}, ...), condition=%wide.region_8.8_spmd, body=%wide.region_5.7_spmd.sunk | while | flops 282656256 | bytes 16038083 | solution.py:112
  150.5 11.7 %while.57 = (s32[]{:T(128)}, bf16[2,512,128]{2,1,0:T(8,128)(2,1)S(1)}, f32[2,2,512]{2,1,0:T(2,128)S(1)}, s32[2]{0:T(128)S(1)}, s32[1024]{0:T(1024)S(1)}, /*index...) while((s32[]{:T(128)}, ...), condition=%wide.region_8.8_spmd, body=%wide.region_5.7_spmd.sunk | while | flops 282656256 | bytes 16038083 | solution.py:112
  165.1 11.7 %while.57 = (s32[]{:T(128)}, bf16[2,512,128]{2,1,0:T(8,128)(2,1)S(1)}, f32[2,2,512]{2,1,0:T(2,128)S(1)}, s32[2]{0:T(128)S(1)}, s32[1024]{0:T(1024)S(1)}, /*index...) while((s32[]{:T(128)}, ...), condition=%wide.region_8.8_spmd, body=%wide.region_5.7_spmd.sunk | while | flops 282656256 | bytes 16038083 | solution.py:112
  177.8 4.8 fusion.81
  182.7 294.4 %while.56 = (s32[]{:T(128)}, f32[6,1024,128]{1,2,0:T(8,128)}, f32[6,1024,128]{1,2,0:T(8,128)}, f32[6,1024,128]{1,2,0:T(8,128)}, bf16[6,1024,128]{1,2,0:T(8,128)(...) while((s32[]{:T(128)}, f32[6,1024,128]{1,2,0:T(8,128)}, ...), condition=%wide.region_14.15_spmd, body=%wide.region_10.14_spmd.sunk | while | flops 689110528 | bytes 80277848 | solution.py:177
  185.9 41.4 %while.58 = (s32[]{:T(128)}, f32[1024,2,64]{0,2,1:T(8,128)}, f32[1024,2,64]{0,2,1:T(8,128)}, f32[2,512,128]{2,1,0:T(8,128)}, s32[2]{0:T(128)S(1)}, /*index=5*/bf...) while((s32[]{:T(128)}, f32[1024,2,64]{0,2,1:T(8,128)}, ...), condition=%wide.region_13.13_spmd.clone, body=%wide.region_11.12_spmd.clone.sunk | while | flops 689110528 | bytes 61385688 | solution.py:168
  192.7 4.1 multiply_reduce_fusion.2
  202.1 4.4 fusion.144
  222.8 4.5 fusion.144
  235.0 41.3 %while.58 = (s32[]{:T(128)}, f32[1024,2,64]{0,2,1:T(8,128)}, f32[1024,2,64]{0,2,1:T(8,128)}, f32[2,512,128]{2,1,0:T(8,128)}, s32[2]{0:T(128)S(1)}, /*index=5*/bf...) while((s32[]{:T(128)}, f32[1024,2,64]{0,2,1:T(8,128)}, ...), condition=%wide.region_13.13_spmd.clone, body=%wide.region_11.12_spmd.clone.sunk | while | flops 689110528 | bytes 61385688 | solution.py:168
  251.1 4.4 fusion.144
  271.8 4.5 fusion.144
  284.1 41.3 %while.58 = (s32[]{:T(128)}, f32[1024,2,64]{0,2,1:T(8,128)}, f32[1024,2,64]{0,2,1:T(8,128)}, f32[2,512,128]{2,1,0:T(8,128)}, s32[2]{0:T(128)S(1)}, /*index=5*/bf...) while((s32[]{:T(128)}, f32[1024,2,64]{0,2,1:T(8,128)}, ...), condition=%wide.region_13.13_spmd.clone, body=%wide.region_11.12_spmd.clone.sunk | while | flops 689110528 | bytes 61385688 | solution.py:168
  300.2 4.4 fusion.144
  320.9 4.5 fusion.144
  333.1 41.3 %while.58 = (s32[]{:T(128)}, f32[1024,2,64]{0,2,1:T(8,128)}, f32[1024,2,64]{0,2,1:T(8,128)}, f32[2,512,128]{2,1,0:T(8,128)}, s32[2]{0:T(128)S(1)}, /*index=5*/bf...) while((s32[]{:T(128)}, f32[1024,2,64]{0,2,1:T(8,128)}, ...), condition=%wide.region_13.13_spmd.clone, body=%wide.region_11.12_spmd.clone.sunk | while | flops 689110528 | bytes 61385688 | solution.py:168
  349.3 4.4 fusion.144
  360.4 4.1 multiply_reduce_fusion.2
  370.0 4.5 fusion.144
  382.2 41.3 %while.58 = (s32[]{:T(128)}, f32[1024,2,64]{0,2,1:T(8,128)}, f32[1024,2,64]{0,2,1:T(8,128)}, f32[2,512,128]{2,1,0:T(8,128)}, s32[2]{0:T(128)S(1)}, /*index=5*/bf...) while((s32[]{:T(128)}, f32[1024,2,64]{0,2,1:T(8,128)}, ...), condition=%wide.region_13.13_spmd.clone, body=%wide.region_11.12_spmd.clone.sunk | while | flops 689110528 | bytes 61385688 | solution.py:168
  398.3 4.4 fusion.144
  409.5 4.1 multiply_reduce_fusion.2
  419.0 4.5 fusion.144
  431.3 41.3 %while.58 = (s32[]{:T(128)}, f32[1024,2,64]{0,2,1:T(8,128)}, f32[1024,2,64]{0,2,1:T(8,128)}, f32[2,512,128]{2,1,0:T(8,128)}, s32[2]{0:T(128)S(1)}, /*index=5*/bf...) while((s32[]{:T(128)}, f32[1024,2,64]{0,2,1:T(8,128)}, ...), condition=%wide.region_13.13_spmd.clone, body=%wide.region_11.12_spmd.clone.sunk | while | flops 689110528 | bytes 61385688 | solution.py:168
  447.4 4.4 fusion.144
  468.1 4.5 fusion.144
  488.0 6.6 fusion.75
  495.3 5.2 all-gather
  500.6 36.6 %multiply_convert_fusion.1 = (bf16[1024,3072]{1,0:T(8,128)(2,1)}, f32[1024,3072]{1,0:T(8,128)}, f32[1024,3072]{1,0:T(8,128)}) fusion(f32[3072]{0:T(1024)S(1)} %bitcast.185, bf16[768,3072]{1,0:T(8,128)(2,1)} %all-gather.10.cloned.1.call-done, bf16[1024,768]{1,0:T(8,128)(2,1)S(1)} %copy-done.8, f32[768]{0:T(1024)S(1)} %convert_element_type.110, ...), kind=kOutput, calls=%fused_computation.63 | convolution fusion | flops 5044174848 | bytes 37775360 | tf_op jit(solution)/shard_map/dot_general | solution.py:247
  537.1 16.9 %convert_reduce_fusion = (f32[3072]{0:T(1024)S(1)}, bf16[1024,3072]{1,0:T(8,128)(2,1)}) fusion(f32[1024,3072]{1,0:T(8,128)} %get-tuple-element.389, bf16[3072,768]{1,0:T(8,128)(2,1)} %all-gather.12.cloned.1.call-done, bf16[1024,768]{1,0:T(8,128)(2,1)S(1)} %copy-done.19, pred[1024]{0:T(1024)(128)(4,1)S(1)} %copy-done.37, ...), kind=kOutput, calls=%fused_computation.61 | convolution fusion | flops 4886098944 | bytes 37774336 | tf_op jit(solution)/shard_map/dot_general | solution.py:61
  554.1 10.6 %fusion.71 = f32[768,3072]{1,0:T(8,128)} fusion(bf16[1024,3072]{1,0:T(8,128)(2,1)} %get-tuple-element.427, bf16[1024,768]{1,0:T(8,128)(2,1)S(1)} %copy-done.8, f32[768]{0:T(1024)S(1)} %convert_element_type.110, f32[768]{0:T(1024)S(1)} %convert_element_type.109, f32[1024]{0:T(1024)S(1)} %copy-done.32, f32[1024]{0:T(1024)S(1)} %copy-done.27), kind=kOutput, calls=%fused_computation.156 | convolution fusion | flops 4836556800 | bytes 17315840 | tf_op jit(solution)/shard_map/dot_general | solution.py:55
  564.8 11.0 %fusion.80 = f32[3072,768]{1,0:T(8,128)} fusion(bf16[1024,3072]{1,0:T(8,128)(2,1)} %get-tuple-element.388, bf16[1024,768]{1,0:T(8,128)(2,1)S(1)} %copy-done.19, pred[1024]{0:T(1024)(128)(4,1)S(1)} %copy-done.37), kind=kOutput, calls=%fused_computation.161 | convolution fusion | flops 4832624640 | bytes 17302528 | tf_op jit(solution)/shard_map/dot_general | solution.py:55
  575.9 69.1 %reduce-scatter.9.cloned.1.call-done = f32[192,3072]{1,0:T(8,128)} async-done(((f32[768,3072]{1,0:T(8,128)}), f32[192,3072]{1,0:T(8,128)}) %reduce-scatter.9.cloned.1.call-update) | async-done | bytes 2359312 | tf_op jit(solution)/shard_map/reduce_scatter | solution.py:301
  645.0 81.1 %reduce-scatter.11.cloned.1.call-done = f32[768,768]{1,0:T(8,128)} async-done(((f32[3072,768]{1,0:T(8,128)}), f32[768,768]{1,0:T(8,128)}) %reduce-scatter.11.cloned.1.call-update) | async-done | bytes 2359312 | tf_op jit(solution)/shard_map/reduce_scatter | solution.py:303
  728.1 9.0 fusion.89
  737.1 7.0 fusion.83
  750.6 11.7 %all-reduce.27 = (f32[768]{0:T(1024)S(1)}, f32[768]{0:T(1024)S(1)}, f32[768]{0:T(1024)S(1)}, f32[768]{0:T(1024)S(1)}, f32[2304]{0:T(1024)S(1)}, /*index=5*/f32[768]{0:T(1024)S(1)}, f32[3072]{0:T(1024)S(1)}) all-reduce(f32[768]{0:T(1024)S(1)} %get-tuple-element.288, ...), channel_id=2, replica_groups=mesh['rep'=8,'shard'=4] {'shard'}, use_global_device_ids=true, to_apply=%region_20.21.clone | all-reduce | flops 9216 | bytes 73728
  762.9 39.8 %all-reduce.25 = (f32[192]{0:T(256)}, f32[192]{0:T(256)}, f32[192]{0:T(256)}, f32[192]{0:T(256)}, f32[576]{0:T(1024)}, /*index=5*/f32[192]{0:T(256)S(1)}, f32[768]{0:T(1024)}) all-reduce(f32[192]{0:T(256)S(1)} %dynamic-slice.8, f32[192]{0:T(256)S(1)} %dynamic-slice.10, ...), channel_id=1, replica_groups=mesh['rep'=8,'shard'=4] {'rep'}, use_global_device_ids=true, to_apply=%region_21.22 | all-reduce | flops 2304 | bytes 18432 | tf_op jit(solution)/shard_map/psum | solution.py:306
  802.7 8.7 fusion.88
  814.2 152.7 %all-reduce.31.cloned.1.call-done = (f32[192,2304]{1,0:T(8,128)}, f32[192,768]{1,0:T(8,128)}, f32[192,3072]{1,0:T(8,128)}, f32[768,768]{1,0:T(8,128)}) async-done(((f32[192,2304]{1,0:T(8,128)}, f32[192,768]{1,0:T(8,128)}, f32[192,3072]{1,0:T(8,128)}, f32[768,768]{1,0:T(8,128)}), (f32[192,2304]{1,0:T(8,128)}, f32[192,768]{1,0:T(8,128)}, f32[192,3072]{1,0:T(8,128)}, ...) | async-done | bytes 7077904 | tf_op jit(solution)/shard_map/psum | solution.py:306
  (773 shorter events, 323.0 us)
Async XLA Ops:
  7.3 21.3 %copy-start.7 = (bf16[1024,768]{1,0:T(8,128)(2,1)S(1)}, bf16[1024,768]{1,0:T(8,128)(2,1)}, u32[]{:S(2)}) copy-start(bf16[1024,768]{1,0:T(8,128)(2,1)} %param.23) | copy-start | bytes 4718596
  7.3 23.1 %all-gather.8.cloned.1.call-start = ((), (), s32[]{:S(2)}) async-start(), calls=%async_computation.5 | async-start | bytes 1474560 | tf_op jit(solution)/shard_map/all_gather | solution.py:214
  8.0 54.6 %all-gather.6.cloned.1.call-start = ((), (), s32[]{:S(2)}) async-start(), calls=%async_computation.4 | async-start | bytes 4423680 | tf_op jit(solution)/shard_map/all_gather | solution.py:212
  8.8 21.6 %copy-start.18 = (bf16[1024,768]{1,0:T(8,128)(2,1)S(1)}, bf16[1024,768]{1,0:T(8,128)(2,1)}, u32[]{:S(2)}) copy-start(bf16[1024,768]{1,0:T(8,128)(2,1)} %param.25) | copy-start | bytes 4718596
  8.8 491.7 %all-gather.10.cloned.1.call-start = ((), (), s32[]{:S(2)}) async-start(), calls=%async_computation.6 | async-start | bytes 5898240 | tf_op jit(solution)/shard_map/all_gather | solution.py:216
  9.5 527.6 %all-gather.12.cloned.1.call-start = ((), (), s32[]{:S(2)}) async-start(), calls=%async_computation.7 | async-start | bytes 5898240 | tf_op jit(solution)/shard_map/all_gather | solution.py:218
  10.1 565.8 %reduce-scatter.7.cloned.1.call-start = ((), (), s32[]{:S(2)}) async-start(), calls=%async_computation.9 | async-start | bytes 2949120 | tf_op jit(solution)/shard_map/reduce_scatter | solution.py:299
  10.3 24.1 %copy-start.35 = (pred[1024]{0:T(1024)(128)(4,1)}, pred[1024]{0:T(1024)(128)(4,1)S(1)}, u32[]{:S(2)}) copy-start(pred[1024]{0:T(1024)(128)(4,1)S(1)} %broadcast_compare_fusion) | copy-start | bytes 3076
  28.5 34.1 %copy-start.28 = (f32[768]{0:T(1024)}, f32[768]{0:T(1024)S(1)}, u32[]{:S(2)}) copy-start(f32[768]{0:T(1024)S(1)} %convert_element_type.100) | copy-start | bytes 9220
  28.5 34.1 %copy-start.38 = (f32[768]{0:T(1024)}, f32[768]{0:T(1024)S(1)}, u32[]{:S(2)}) copy-start(f32[768]{0:T(1024)S(1)} %convert_element_type.101) | copy-start | bytes 9220
  28.8 33.8 %copy-start.26 = (f32[1024]{0:T(1024)}, f32[1024]{0:T(1024)S(1)}, u32[]{:S(2)}) copy-start(f32[1024]{0:T(1024)S(1)} %broadcast_multiply_fusion.1) | copy-start | bytes 12292
  29.5 33.1 %copy-start.31 = (f32[1024]{0:T(1024)}, f32[1024]{0:T(1024)S(1)}, u32[]{:S(2)}) copy-start(f32[1024]{0:T(1024)S(1)} %fusion.70) | copy-start | bytes 12292
  30.4 56.9 %copy-start.20 = (f32[1024,16]{0,1:T(8,128)}, f32[1024,16]{0,1:T(8,128)S(1)}, u32[]{:S(2)}) copy-start(f32[1024,16]{0,1:T(8,128)S(1)} %get-tuple-element.418) | copy-start | bytes 196612
  30.4 56.9 %copy-start.22 = (f32[1024,16]{0,1:T(8,128)}, f32[1024,16]{0,1:T(8,128)S(1)}, u32[]{:S(2)}) copy-start(f32[1024,16]{0,1:T(8,128)S(1)} %get-tuple-element.419) | copy-start | bytes 196612
  90.1 87.7 %copy-start.36 = (pred[1024]{0:T(1024)(128)(4,1)S(1)}, pred[1024]{0:T(1024)(128)(4,1)}, u32[]{:S(2)}) copy-start(pred[1024]{0:T(1024)(128)(4,1)} %copy-done.35) | copy-start | bytes 3076
  182.6 393.3 %reduce-scatter.5.cloned.1.call-start = ((), (), s32[]{:S(2)}) async-start(), calls=%async_computation.8 | async-start | bytes 8847360 | tf_op jit(solution)/shard_map/reduce_scatter | solution.py:297
  185.9 10.9 %copy-start.1 = (bf16[1024,2,64]{0,2,1:T(8,128)(2,1)}, bf16[1024,2,64]{0,2,1:T(8,128)(2,1)S(1)}, u32[]{:S(2)}) copy-start(bf16[1024,2,64]{0,2,1:T(8,128)(2,1)S(1)} %get-tuple-element.753) | copy-start | bytes 786436 | tf_op jit(solution)/shard_map/while/body/eval_jaxpr/while
  185.9 10.9 %copy-start.3 = (bf16[1024,2,64]{0,2,1:T(8,128)(2,1)}, bf16[1024,2,64]{0,2,1:T(8,128)(2,1)S(1)}, u32[]{:S(2)}) copy-start(bf16[1024,2,64]{0,2,1:T(8,128)(2,1)S(1)} %get-tuple-element.758) | copy-start | bytes 786436 | tf_op jit(solution)/shard_map/while/body/eval_jaxpr/while
  186.0 10.9 %copy-start.5 = (bf16[1024,2,64]{0,2,1:T(8,128)(2,1)}, bf16[1024,2,64]{0,2,1:T(8,128)(2,1)S(1)}, u32[]{:S(2)}) copy-start(bf16[1024,2,64]{0,2,1:T(8,128)(2,1)S(1)} %get-tuple-element.757) | copy-start | bytes 786436 | tf_op jit(solution)/shard_map/while/body/eval_jaxpr/while
  206.5 10.9 %copy-start.1 = (bf16[1024,2,64]{0,2,1:T(8,128)(2,1)}, bf16[1024,2,64]{0,2,1:T(8,128)(2,1)S(1)}, u32[]{:S(2)}) copy-start(bf16[1024,2,64]{0,2,1:T(8,128)(2,1)S(1)} %get-tuple-element.753) | copy-start | bytes 786436 | tf_op jit(solution)/shard_map/while/body/eval_jaxpr/while
  206.5 10.9 %copy-start.3 = (bf16[1024,2,64]{0,2,1:T(8,128)(2,1)}, bf16[1024,2,64]{0,2,1:T(8,128)(2,1)S(1)}, u32[]{:S(2)}) copy-start(bf16[1024,2,64]{0,2,1:T(8,128)(2,1)S(1)} %get-tuple-element.758) | copy-start | bytes 786436 | tf_op jit(solution)/shard_map/while/body/eval_jaxpr/while
  206.5 10.9 %copy-start.5 = (bf16[1024,2,64]{0,2,1:T(8,128)(2,1)}, bf16[1024,2,64]{0,2,1:T(8,128)(2,1)S(1)}, u32[]{:S(2)}) copy-start(bf16[1024,2,64]{0,2,1:T(8,128)(2,1)S(1)} %get-tuple-element.757) | copy-start | bytes 786436 | tf_op jit(solution)/shard_map/while/body/eval_jaxpr/while
  255.6 10.9 %copy-start.1 = (bf16[1024,2,64]{0,2,1:T(8,128)(2,1)}, bf16[1024,2,64]{0,2,1:T(8,128)(2,1)S(1)}, u32[]{:S(2)}) copy-start(bf16[1024,2,64]{0,2,1:T(8,128)(2,1)S(1)} %get-tuple-element.753) | copy-start | bytes 786436 | tf_op jit(solution)/shard_map/while/body/eval_jaxpr/while
  255.6 10.9 %copy-start.3 = (bf16[1024,2,64]{0,2,1:T(8,128)(2,1)}, bf16[1024,2,64]{0,2,1:T(8,128)(2,1)S(1)}, u32[]{:S(2)}) copy-start(bf16[1024,2,64]{0,2,1:T(8,128)(2,1)S(1)} %get-tuple-element.758) | copy-start | bytes 786436 | tf_op jit(solution)/shard_map/while/body/eval_jaxpr/while
  255.6 10.9 %copy-start.5 = (bf16[1024,2,64]{0,2,1:T(8,128)(2,1)}, bf16[1024,2,64]{0,2,1:T(8,128)(2,1)S(1)}, u32[]{:S(2)}) copy-start(bf16[1024,2,64]{0,2,1:T(8,128)(2,1)S(1)} %get-tuple-element.757) | copy-start | bytes 786436 | tf_op jit(solution)/shard_map/while/body/eval_jaxpr/while
  284.1 10.9 %copy-start.1 = (bf16[1024,2,64]{0,2,1:T(8,128)(2,1)}, bf16[1024,2,64]{0,2,1:T(8,128)(2,1)S(1)}, u32[]{:S(2)}) copy-start(bf16[1024,2,64]{0,2,1:T(8,128)(2,1)S(1)} %get-tuple-element.753) | copy-start | bytes 786436 | tf_op jit(solution)/shard_map/while/body/eval_jaxpr/while
  304.6 10.9 %copy-start.1 = (bf16[1024,2,64]{0,2,1:T(8,128)(2,1)}, bf16[1024,2,64]{0,2,1:T(8,128)(2,1)S(1)}, u32[]{:S(2)}) copy-start(bf16[1024,2,64]{0,2,1:T(8,128)(2,1)S(1)} %get-tuple-element.753) | copy-start | bytes 786436 | tf_op jit(solution)/shard_map/while/body/eval_jaxpr/while
  304.6 10.9 %copy-start.3 = (bf16[1024,2,64]{0,2,1:T(8,128)(2,1)}, bf16[1024,2,64]{0,2,1:T(8,128)(2,1)S(1)}, u32[]{:S(2)}) copy-start(bf16[1024,2,64]{0,2,1:T(8,128)(2,1)S(1)} %get-tuple-element.758) | copy-start | bytes 786436 | tf_op jit(solution)/shard_map/while/body/eval_jaxpr/while
  304.6 10.9 %copy-start.5 = (bf16[1024,2,64]{0,2,1:T(8,128)(2,1)}, bf16[1024,2,64]{0,2,1:T(8,128)(2,1)S(1)}, u32[]{:S(2)}) copy-start(bf16[1024,2,64]{0,2,1:T(8,128)(2,1)S(1)} %get-tuple-element.757) | copy-start | bytes 786436 | tf_op jit(solution)/shard_map/while/body/eval_jaxpr/while
  333.2 10.9 %copy-start.1 = (bf16[1024,2,64]{0,2,1:T(8,128)(2,1)}, bf16[1024,2,64]{0,2,1:T(8,128)(2,1)S(1)}, u32[]{:S(2)}) copy-start(bf16[1024,2,64]{0,2,1:T(8,128)(2,1)S(1)} %get-tuple-element.753) | copy-start | bytes 786436 | tf_op jit(solution)/shard_map/while/body/eval_jaxpr/while
  333.2 10.9 %copy-start.3 = (bf16[1024,2,64]{0,2,1:T(8,128)(2,1)}, bf16[1024,2,64]{0,2,1:T(8,128)(2,1)S(1)}, u32[]{:S(2)}) copy-start(bf16[1024,2,64]{0,2,1:T(8,128)(2,1)S(1)} %get-tuple-element.758) | copy-start | bytes 786436 | tf_op jit(solution)/shard_map/while/body/eval_jaxpr/while
  333.2 10.9 %copy-start.5 = (bf16[1024,2,64]{0,2,1:T(8,128)(2,1)}, bf16[1024,2,64]{0,2,1:T(8,128)(2,1)S(1)}, u32[]{:S(2)}) copy-start(bf16[1024,2,64]{0,2,1:T(8,128)(2,1)S(1)} %get-tuple-element.757) | copy-start | bytes 786436 | tf_op jit(solution)/shard_map/while/body/eval_jaxpr/while
  353.7 10.9 %copy-start.1 = (bf16[1024,2,64]{0,2,1:T(8,128)(2,1)}, bf16[1024,2,64]{0,2,1:T(8,128)(2,1)S(1)}, u32[]{:S(2)}) copy-start(bf16[1024,2,64]{0,2,1:T(8,128)(2,1)S(1)} %get-tuple-element.753) | copy-start | bytes 786436 | tf_op jit(solution)/shard_map/while/body/eval_jaxpr/while
  353.7 10.9 %copy-start.3 = (bf16[1024,2,64]{0,2,1:T(8,128)(2,1)}, bf16[1024,2,64]{0,2,1:T(8,128)(2,1)S(1)}, u32[]{:S(2)}) copy-start(bf16[1024,2,64]{0,2,1:T(8,128)(2,1)S(1)} %get-tuple-element.758) | copy-start | bytes 786436 | tf_op jit(solution)/shard_map/while/body/eval_jaxpr/while
  353.7 10.9 %copy-start.5 = (bf16[1024,2,64]{0,2,1:T(8,128)(2,1)}, bf16[1024,2,64]{0,2,1:T(8,128)(2,1)S(1)}, u32[]{:S(2)}) copy-start(bf16[1024,2,64]{0,2,1:T(8,128)(2,1)S(1)} %get-tuple-element.757) | copy-start | bytes 786436 | tf_op jit(solution)/shard_map/while/body/eval_jaxpr/while
  402.7 10.9 %copy-start.1 = (bf16[1024,2,64]{0,2,1:T(8,128)(2,1)}, bf16[1024,2,64]{0,2,1:T(8,128)(2,1)S(1)}, u32[]{:S(2)}) copy-start(bf16[1024,2,64]{0,2,1:T(8,128)(2,1)S(1)} %get-tuple-element.753) | copy-start | bytes 786436 | tf_op jit(solution)/shard_map/while/body/eval_jaxpr/while
  402.7 10.9 %copy-start.3 = (bf16[1024,2,64]{0,2,1:T(8,128)(2,1)}, bf16[1024,2,64]{0,2,1:T(8,128)(2,1)S(1)}, u32[]{:S(2)}) copy-start(bf16[1024,2,64]{0,2,1:T(8,128)(2,1)S(1)} %get-tuple-element.758) | copy-start | bytes 786436 | tf_op jit(solution)/shard_map/while/body/eval_jaxpr/while
  402.7 10.9 %copy-start.5 = (bf16[1024,2,64]{0,2,1:T(8,128)(2,1)}, bf16[1024,2,64]{0,2,1:T(8,128)(2,1)S(1)}, u32[]{:S(2)}) copy-start(bf16[1024,2,64]{0,2,1:T(8,128)(2,1)S(1)} %get-tuple-element.757) | copy-start | bytes 786436 | tf_op jit(solution)/shard_map/while/body/eval_jaxpr/while
  431.3 10.9 %copy-start.1 = (bf16[1024,2,64]{0,2,1:T(8,128)(2,1)}, bf16[1024,2,64]{0,2,1:T(8,128)(2,1)S(1)}, u32[]{:S(2)}) copy-start(bf16[1024,2,64]{0,2,1:T(8,128)(2,1)S(1)} %get-tuple-element.753) | copy-start | bytes 786436 | tf_op jit(solution)/shard_map/while/body/eval_jaxpr/while
  451.8 10.9 %copy-start.1 = (bf16[1024,2,64]{0,2,1:T(8,128)(2,1)}, bf16[1024,2,64]{0,2,1:T(8,128)(2,1)S(1)}, u32[]{:S(2)}) copy-start(bf16[1024,2,64]{0,2,1:T(8,128)(2,1)S(1)} %get-tuple-element.753) | copy-start | bytes 786436 | tf_op jit(solution)/shard_map/while/body/eval_jaxpr/while
  451.8 10.9 %copy-start.3 = (bf16[1024,2,64]{0,2,1:T(8,128)(2,1)}, bf16[1024,2,64]{0,2,1:T(8,128)(2,1)S(1)}, u32[]{:S(2)}) copy-start(bf16[1024,2,64]{0,2,1:T(8,128)(2,1)S(1)} %get-tuple-element.758) | copy-start | bytes 786436 | tf_op jit(solution)/shard_map/while/body/eval_jaxpr/while
  451.8 10.9 %copy-start.5 = (bf16[1024,2,64]{0,2,1:T(8,128)(2,1)}, bf16[1024,2,64]{0,2,1:T(8,128)(2,1)S(1)}, u32[]{:S(2)}) copy-start(bf16[1024,2,64]{0,2,1:T(8,128)(2,1)S(1)} %get-tuple-element.757) | copy-start | bytes 786436 | tf_op jit(solution)/shard_map/while/body/eval_jaxpr/while
  494.7 150.3 %reduce-scatter.9.cloned.1.call-start = ((), (), s32[]{:S(2)}) async-start(), calls=%async_computation.10 | async-start | bytes 11796480 | tf_op jit(solution)/shard_map/reduce_scatter | solution.py:301
  500.5 36.6 %copy-start.19 = (bf16[1024,768]{1,0:T(8,128)(2,1)S(1)}, bf16[1024,768]{1,0:T(8,128)(2,1)}, u32[]{:S(2)}) copy-start(bf16[1024,768]{1,0:T(8,128)(2,1)} %param.25) | copy-start | bytes 4718596
  500.5 36.6 %copy-start.37 = (pred[1024]{0:T(1024)(128)(4,1)S(1)}, pred[1024]{0:T(1024)(128)(4,1)}, u32[]{:S(2)}) copy-start(pred[1024]{0:T(1024)(128)(4,1)} %copy-done.35) | copy-start | bytes 3076
  564.7 161.3 %reduce-scatter.11.cloned.1.call-start = ((), (), s32[]{:S(2)}) async-start(), calls=%async_computation.11 | async-start | bytes 11796480 | tf_op jit(solution)/shard_map/reduce_scatter | solution.py:303
  575.8 391.1 %all-reduce.31.cloned.1.call-start = ((), (), s32[]{:S(2)}) async-start(), calls=%async_computation.12 | async-start | bytes 14155776 | tf_op jit(solution)/shard_map/psum | solution.py:306
  802.7 164.2 %copy-start.47 = (f32[192]{0:T(256)}, f32[192]{0:T(256)S(1)}, u32[]{:S(2)}) copy-start(f32[192]{0:T(256)S(1)} %get-tuple-element.927) | copy-start | bytes 2308
  (105 other events, 506.5 us)
Sparse Core Ops, SparseCore 0:
  9.7 20.5 all-gather.7
  31.8 30.7 all-gather.5
  64.2 37.4 all-gather.9
  103.1 37.4 all-gather.11
  182.7 33.2 reduce-scatter.6
  494.8 63.8 reduce-scatter.4
  564.9 80.0 reduce-scatter.8
  647.6 78.4 reduce-scatter.10
  730.5 236.4 all-reduce.30
where the time goes:
time: 986 us; the launch traced here: 981 us
  waiting for transfers between devices  334 us (34%)
  matrix products  330 us (33%)
  local copies, waits for them, and re-layouts  128 us (13%)
  blocking collectives  71.3 us (7%)
  other arithmetic  58.1 us (6%)
  loops' own time  42.1 us (4%)
  between operations  18.3 us (2%)
    psum x1, waiting for transfers between devices, local(): lax.psum((shares[0], shares[1], shares[2], shares[3], shares[4], shares[5...  153 us
    reduce_scatter x1, waiting for transfers between devices, local(): lax.psum_scatter(grad_down, 'shard', scatter_dimension=0, tiled=True)  81.1 us
    reduce_scatter x1, waiting for transfers between devices, local(): lax.psum_scatter(grad_up, 'shard', scatter_dimension=0, tiled=True)  69.1 us
    dot_general x12, matrix products, advance(): jnp.einsum('hqk,qhd->khd', weights_low, grad_block, preferred_element_typ...  53.4 us
    dot_general x12, matrix products, advance(): jnp.einsum('qhd,khd->hqk', grad_block, value_h, preferred_element_type=jn...  49.5 us
    psum x1, blocking collectives, local(): lax.psum((shares[0], shares[1], shares[2], shares[3], shares[4], shares[5...  39.8 us
    dot_general x4, matrix products, across(): lax.dot_general(left, right, (((1,), (1,)), ((), ())), preferred_element_...  36.9 us
    dot_general x1, matrix products, local(): upward = jnp.dot(second_in, w_up, preferred_element_type=jnp.float32) + b_up  36.6 us
  transfers between devices with their start and end apart: 9, of which 4 were waited for; matrix products, arithmetic and copies ran while one was open for 51% of the time, Pallas kernels for 0%

commit v1 on v0

v1 whole, which is shorter than its diff:
```python
import functools

import jax
import jax.numpy as jnp
from jax import lax
from jax.experimental import pallas as pl
from jax.experimental.pallas import tpu as pltpu
from jax.sharding import PartitionSpec as P

D = 768
HEADS = 12
HEAD_DIM = 64
ROTARY = 16
EPS = 1e-05
PAIR = 2 * HEAD_DIM
PAIRS = HEADS // 2
VMEM_BYTES = 56 * 1024 * 1024
F32 = jnp.float32
BF16 = jnp.bfloat16


def positions(segments):
    slot_index = jnp.arange(segments.shape[0], dtype=jnp.int32)
    is_start = jnp.concatenate([jnp.ones((1,), bool), segments[1:] != segments[:-1]])
    seq_start = lax.cummax(jnp.where(is_start, slot_index, jnp.zeros_like(slot_index)), axis=0)
    return slot_index - seq_start


def turn_tables(places):
    half = ROTARY // 2
    length = places.shape[0]
    rates = 10000.0 ** (-(jnp.arange(half, dtype=F32) * 2.0) / ROTARY)
    turned = places.astype(F32)[:, None] * rates[None, :]
    cosine, sine = jnp.cos(turned), jnp.sin(turned)
    rest = HEAD_DIM - ROTARY
    zero_half = jnp.zeros((length, half), F32)
    zeros = jnp.zeros((length, rest), F32)
    keep = jnp.concatenate([cosine, cosine, jnp.ones((length, rest), F32)], -1)
    ahead = jnp.concatenate([-sine, zero_half, zeros], -1)
    behind = jnp.concatenate([zero_half, sine, zeros], -1)
    return tuple(jnp.concatenate([item, item], -1) for item in (keep, ahead, behind))


def contract_rows(left, right):
    return lax.dot_general(left, right, (((0,), (0,)), ((), ())), preferred_element_type=F32)


def across(left, right):
    return lax.dot_general(left, right, (((1,), (1,)), ((), ())), preferred_element_type=F32)


def dot(left, right):
    return jnp.dot(left, right, preferred_element_type=F32)


def attention_kernel(
    rows,
    a1_ref,
    dy_ref,
    wq_ref,
    wk_ref,
    wv_ref,
    bq_ref,
    bk_ref,
    bv_ref,
    wo_ref,
    keep_ref,
    ahead_ref,
    behind_ref,
    seg_col_ref,
    seg_row_ref,
    o_ref,
    dqkv_ref,
    bias_ref,
    dkt_ref,
    dvt_ref,
):
    number = pl.program_id(0)
    length = a1_ref.shape[0]
    half = ROTARY // 2

    @pl.when(number == 0)
    def _():
        row_id = lax.broadcasted_iota(jnp.int32, (length, length), 0)
        col_id = lax.broadcasted_iota(jnp.int32, (length, length), 1)
        readable = (seg_col_ref[...] == seg_row_ref[...]) & (row_id >= col_id)
        bias_ref[...] = jnp.where(readable, 0.0, -1e30)

    keep, ahead, behind = keep_ref[...], ahead_ref[...], behind_ref[...]

    def turn(u):
        return (
            u * keep
            + pltpu.roll(u, PAIR - half, 1) * ahead
            + pltpu.roll(u, half, 1) * behind
        )

    def turn_back(g):
        return (
            g * keep
            + pltpu.roll(g * ahead, half, 1)
            + pltpu.roll(g * behind, PAIR - half, 1)
        )

    a1 = a1_ref[...]
    q = (turn(dot(a1, wq_ref[...]) + bq_ref[...])).astype(BF16)
    q = (q.astype(F32) * 0.125)
    k = (turn(dot(a1, wk_ref[...]) + bk_ref[...])).astype(BF16).astype(F32)
    v = (dot(a1, wv_ref[...]) + bv_ref[...]).astype(BF16).astype(F32)
    do = across(dy_ref[...], wo_ref[...]).astype(BF16).astype(F32)
    lane = lax.broadcasted_iota(jnp.int32, (length, PAIR), 1)
    first = lane < HEAD_DIM
    zero = jnp.zeros_like(q)

    def split(item):
        return (
            jnp.where(first, item, zero).astype(BF16),
            jnp.where(first, zero, item).astype(BF16),
        )

    q_of, k_of, v_of, do_of = split(q), split(k), split(v), split(do)
    qt, kt = jnp.transpose(q).astype(BF16), jnp.transpose(k).astype(BF16)
    vt, dot_t = jnp.transpose(v).astype(BF16), jnp.transpose(do).astype(BF16)
    dkt_ref[...] = jnp.zeros_like(dkt_ref)
    dvt_ref[...] = jnp.zeros_like(dvt_ref)
    dq_parts = []
    for block in range(length // rows):
        lo, hi = block * rows, (block + 1) * rows
        bias = bias_ref[lo:hi, :hi]
        out = None
        dq = None
        for head in range(2):
            h0, h1 = head * HEAD_DIM, (head + 1) * HEAD_DIM
            scores = dot(q_of[head][lo:hi], kt[:, :hi]) + bias
            raised = jnp.exp(scores - jnp.max(scores, -1, keepdims=True))
            weights = raised * (1.0 / jnp.sum(raised, -1, keepdims=True))
            low = weights.astype(BF16)
            part = dot(low, v_of[head][:hi])
            out = part if out is None else out + part
            dvt_ref[h0:h1, :hi] += dot(dot_t[h0:h1, lo:hi], low)
            grad_w = dot(do_of[head][lo:hi], vt[:, :hi])
            prod = weights * grad_w
            centre = jnp.sum(prod, -1, keepdims=True)
            grad_s = (prod - weights * centre).astype(BF16)
            part = dot(grad_s, k_of[head][:hi])
            dq = part if dq is None else dq + part
            dkt_ref[h0:h1, :hi] += dot(qt[h0:h1, lo:hi], grad_s)
        o_ref[lo:hi, :] = out.astype(BF16)
        dq_parts.append(dq * 0.125)
    dq = turn_back(jnp.concatenate(dq_parts, 0))
    dk = turn_back(jnp.transpose(dkt_ref[...]))
    dv = jnp.transpose(dvt_ref[...])
    for index, item in enumerate((dq, dk, dv)):
        spot = pl.multiple_of(index * D + number * PAIR, PAIR)
        dqkv_ref[:, pl.ds(spot, PAIR)] = item.astype(BF16)


def attention(a1, dy, w_qkv, b_qkv, w_out, tables, segments):
    length = a1.shape[0]
    whole = lambda shape: pl.BlockSpec(shape, lambda j: (0, 0))
    column = lambda shift: pl.BlockSpec((D, PAIR), lambda j: (0, shift + j))
    bias = lambda shift: pl.BlockSpec((1, PAIR), lambda j: (0, shift + j))
    b_row = b_qkv.reshape(1, 3 * D)
    return pl.pallas_call(
        functools.partial(attention_kernel, 256),
        grid=(PAIRS,),
        out_shape=(
            jax.ShapeDtypeStruct((length, D), BF16),
            jax.ShapeDtypeStruct((length, 3 * D), BF16),
        ),
        in_specs=[
            whole((length, D)),
            whole((length, D)),
            column(0),
            column(PAIRS),
            column(2 * PAIRS),
            bias(0),
            bias(PAIRS),
            bias(2 * PAIRS),
            pl.BlockSpec((PAIR, D), lambda j: (j, 0)),
            whole((length, PAIR)),
            whole((length, PAIR)),
            whole((length, PAIR)),
            whole((length, 1)),
            whole((1, length)),
        ],
        out_specs=(
            pl.BlockSpec((length, PAIR), lambda j: (0, j)),
            whole((length, 3 * D)),
        ),
        scratch_shapes=[
            pltpu.VMEM((length, length), F32),
            pltpu.VMEM((PAIR, length), F32),
            pltpu.VMEM((PAIR, length), F32),
        ],
        compiler_params=pltpu.CompilerParams(
            dimension_semantics=("arbitrary",), vmem_limit_bytes=VMEM_BYTES
        ),
        cost_estimate=pl.CostEstimate(
            flops=40_000_000_000, bytes_accessed=20_000_000, transcendentals=8_000_000
        ),
    )(
        a1,
        dy,
        w_qkv,
        w_qkv,
        w_qkv,
        b_row,
        b_row,
        b_row,
        w_out,
        *tables,
        segments.reshape(length, 1),
        segments.reshape(1, length),
    )


def feed_kernel(a2_ref, dy_ref, wu_ref, bu_ref, wd_ref, mlp_ref, da2_ref, gu_ref, gd_ref, gb_ref, h_ref, du_ref):
    number = pl.program_id(0)
    length = a2_ref.shape[0]
    step = length // 4

    @pl.when(number == 0)
    def _():
        mlp_ref[...] = jnp.zeros_like(mlp_ref)
        da2_ref[...] = jnp.zeros_like(da2_ref)

    total = None
    for lo in range(0, length, step):
        rows = slice(lo, lo + step)
        u = dot(a2_ref[rows, :], wu_ref[...]) + bu_ref[...]
        area = 0.5 + 0.5 * lax.erf(u * (0.5**0.5))
        h_ref[rows, :] = (u * area).astype(BF16)
        slope = area + u * (jnp.exp(u * u * -0.5) * 0.3989422804014327)
        du = (across(dy_ref[rows, :], wd_ref[...]) * slope).astype(BF16)
        du_ref[rows, :] = du
        part = jnp.sum(du.astype(F32), 0, keepdims=True)
        total = part if total is None else total + part
        mlp_ref[rows, :] += dot(h_ref[rows, :], wd_ref[...])
        da2_ref[rows, :] += across(du, wu_ref[...])
    gb_ref[...] = total
    gu_ref[...] = contract_rows(a2_ref[...], du_ref[...]).astype(gu_ref.dtype)
    gd_ref[...] = contract_rows(h_ref[...], dy_ref[...]).astype(gd_ref.dtype)


def feed(a2, dy, w_up, b_up, w_down):
    length = a2.shape[0]
    width = w_up.shape[1]
    block = 512
    whole = lambda shape: pl.BlockSpec(shape, lambda j: (0, 0))
    return pl.pallas_call(
        feed_kernel,
        grid=(width // block,),
        out_shape=(
            jax.ShapeDtypeStruct((length, D), F32),
            jax.ShapeDtypeStruct((length, D), F32),
            jax.ShapeDtypeStruct((D, width), BF16),
            jax.ShapeDtypeStruct((width, D), BF16),
            jax.ShapeDtypeStruct((1, width), F32),
        ),
        in_specs=[
            whole((length, D)),
            whole((length, D)),
            pl.BlockSpec((D, block), lambda j: (0, j)),
            pl.BlockSpec((1, block), lambda j: (0, j)),
            pl.BlockSpec((block, D), lambda j: (j, 0)),
        ],
        out_specs=(
            whole((length, D)),
            whole((length, D)),
            pl.BlockSpec((D, block), lambda j: (0, j)),
            pl.BlockSpec((block, D), lambda j: (j, 0)),
            pl.BlockSpec((1, block), lambda j: (0, j)),
        ),
        scratch_shapes=[
            pltpu.VMEM((length, block), BF16),
            pltpu.VMEM((length, block), BF16),
        ],
        compiler_params=pltpu.CompilerParams(
            dimension_semantics=("arbitrary",), vmem_limit_bytes=VMEM_BYTES
        ),
        cost_estimate=pl.CostEstimate(
            flops=29_000_000_000, bytes_accessed=30_000_000, transcendentals=6_000_000
        ),
    )(a2, dy, w_up, b_up.reshape(1, width), w_down)


def local(
    hidden_in,
    segment_ids,
    cotangent,
    ln1_gain,
    ln1_bias,
    ln2_gain,
    ln2_bias,
    qkv_weight,
    qkv_bias,
    out_weight,
    out_bias,
    up_weight,
    up_bias,
    down_weight,
    down_bias,
):
    gather = lambda item: lax.all_gather(item, "shard", axis=0, tiled=True)
    vectors = (ln1_gain, ln1_bias, ln2_gain, ln2_bias, qkv_bias, out_bias, up_bias, down_bias)
    sizes = [item.shape[0] for item in vectors]
    offsets = [sum(sizes[:index]) for index in range(len(sizes))]
    group = lax.axis_size("shard")
    packed = gather(jnp.concatenate(vectors)).reshape(group, sum(sizes)).astype(F32)
    gain_one, bias_one, gain_two, bias_two, b_qkv, b_out, b_up, b_down = tuple(
        packed[:, offset : offset + size].reshape(-1) for offset, size in zip(offsets, sizes)
    )
    w_out = gather(out_weight)
    w_qkv = gather(qkv_weight)
    up_weight, down_weight, w_qkv, w_out = lax.optimization_barrier(
        (up_weight, down_weight, w_qkv, w_out)
    )
    w_up = gather(up_weight)
    w_down = gather(down_weight)

    x = hidden_in.astype(F32)
    center = x - jnp.mean(x, -1, keepdims=True)
    scale = lax.rsqrt(jnp.mean(center * center, -1, keepdims=True) + EPS)
    unit = center * scale
    a1 = (unit * gain_one + bias_one).astype(BF16)
    a2 = (unit * gain_two + bias_two).astype(BF16)
    dy = jnp.where((segment_ids >= 0)[:, None], cotangent, jnp.zeros_like(cotangent))
    dy_float = dy.astype(F32)
    tables = turn_tables(positions(segment_ids))

    o, dqkv = attention(a1, dy, w_qkv, b_qkv, w_out, tables, segment_ids)
    scatter = lambda item: lax.psum_scatter(item, "shard", scatter_dimension=0, tiled=True)
    g_qkv = lax.psum(scatter(contract_rows(a1, dqkv).astype(BF16)), "rep")
    g_out = lax.psum(scatter(contract_rows(o, dy).astype(BF16)), "rep")
    mlp, da2, g_up, g_down, g_up_bias = feed(a2, dy, w_up, b_up, w_down)
    g_up, g_down, g_qkv, g_out = lax.optimization_barrier((g_up, g_down, g_qkv, g_out))
    g_up = lax.psum(scatter(g_up), "rep")
    g_down = lax.psum(scatter(g_down), "rep")

    da1 = across(dqkv, w_qkv)
    mixed = (x + (dot(o, w_out) + b_out) + (mlp + b_down)).astype(BF16)
    d_unit = da1 * gain_one + da2 * gain_two
    d_x = scale * (
        d_unit
        - jnp.mean(d_unit, -1, keepdims=True)
        - unit * jnp.mean(d_unit * unit, -1, keepdims=True)
    )
    input_grad = dy_float + d_x
    sum_dy = jnp.sum(dy_float, 0)
    grads = (
        jnp.sum(da1 * unit, 0),
        jnp.sum(da1, 0),
        jnp.sum(da2 * unit, 0),
        jnp.sum(da2, 0),
        jnp.sum(dqkv.astype(F32), 0),
        sum_dy,
        g_up_bias.reshape(-1),
        sum_dy,
    )
    small = jnp.concatenate([item.reshape(group, -1) for item in grads], 1).reshape(-1)
    small = lax.psum(small, ("rep", "shard")).reshape(group, -1)
    mine = lax.dynamic_index_in_dim(small, lax.axis_index("shard"), 0, keepdims=False)
    own = tuple(mine[offset : offset + size] for offset, size in zip(offsets, sizes))
    return (
        mixed,
        input_grad,
        own[0],
        own[1],
        own[2],
        own[3],
        g_qkv.astype(F32),
        own[4],
        g_out.astype(F32),
        own[5],
        g_up.astype(F32),
        own[6],
        g_down.astype(F32),
        own[7],
    )


def solution(mesh):
    tokens = P(("rep", "shard"), None)
    row, matrix = P("shard"), P("shard", None)
    return jax.shard_map(
        local,
        mesh=mesh,
        in_specs=(tokens, P(("rep", "shard")), tokens, row, row, row, row)
        + (matrix, row) * 4,
        out_specs=(tokens, tokens, row, row, row, row) + (matrix, row) * 4,
        check_vma=False,
    )
```

time: 986 us -> 591 us (0.60)
  matrix products: 330 us -> 25.2 us
  local copies, waits for them, and re-layouts: 128 us -> 20 us
  Pallas kernels: 0 us -> 103 us
  loops' own time: 42.1 us -> 0 us
  other arithmetic: 58.1 us -> 22.7 us
  blocking collectives: 71.3 us -> 55.5 us
  waiting for transfers between devices: 334 us -> 348 us
    dot_general x88 -> x1, matrix products: 260 us -> 2.72 us  [dot(): return jnp.dot(left, right, preferred_element_type=F32)]
    pallas_call x0 -> x2, Pallas kernels: none -> 103 us  [the longest x1 67.7 us: attention(): pl.pallas_call(functools.partial(attention_kernel, 256), grid=(PAIRS,), o...]
    all_gather x4, waiting for transfers between devices: 28.2 us -> 93.5 us  [local(): gather = lambda item: lax.all_gather(item, 'shard', axis=0, tiled=True)]
    psum x1 -> x2, waiting for transfers between devices: 153 us -> 96 us  [the longest x1 48.2 us: local(): g_qkv = lax.psum(scatter(contract_rows(a1, dqkv).astype(BF16)), 'rep')]
    dynamic_slice x84 -> x0, local copies, waits for them, and re-layouts: 47.7 us -> none  [the longest x36 30.5 us: attend(): lax.map(one_pair, (to_pairs(query_rows), to_pairs(key_rows), to_pairs(val...]
    dynamic_update_slice x84 -> x0, local copies, waits for them, and re-layouts: 44.2 us -> none  [the longest x18 27 us: attend_back(): lax.map(one_pair, (to_pairs(query_rows), to_pairs(key_rows), to_pairs(val...]
    another operation x14 -> x0, loops' own time: 42.1 us -> none  [the longest x6 32.6 us: one_pair(): lax.scan(advance, (empty, empty), jnp.arange(block_count))]
    dot_general x4 -> x1, matrix products: 36.9 us -> 10.7 us  [across(): lax.dot_general(left, right, (((1,), (1,)), ((), ())), preferred_element_...]
  transfers between devices with their start and end apart: 9 -> 10, of which waited for: 4 -> 9; matrix products, arithmetic and copies ran while one was open for 51% -> 10% of each run, Pallas kernels for 0% -> 6%
where the time goes in v1:
time: 591 us
  waiting for transfers between devices  348 us (59%)
  Pallas kernels  103 us (17%)
  blocking collectives  55.5 us (9%)
  matrix products  25.2 us (4%)
  other arithmetic  22.7 us (4%)
  local copies, waits for them, and re-layouts  20 us (3%)
  between operations  15 us (3%)
    reduce_scatter x4, waiting for transfers between devices, local(): lax.psum_scatter(item, 'shard', scatter_dimension=0, tiled=True)  155 us
    all_gather x4, waiting for transfers between devices, local(): gather = lambda item: lax.all_gather(item, 'shard', axis=0, tiled=True)  93.5 us
    pallas_call x1, Pallas kernels, attention(): pl.pallas_call(functools.partial(attention_kernel, 256), grid=(PAIRS,), o...  67.7 us
    psum x1, waiting for transfers between devices, local(): g_qkv = lax.psum(scatter(contract_rows(a1, dqkv).astype(BF16)), 'rep')  48.2 us
    psum x1, waiting for transfers between devices, local(): g_up = lax.psum(scatter(g_up), 'rep')  47.8 us
    psum x1, blocking collectives, local(): small = lax.psum(small, ('rep', 'shard')).reshape(group, -1)  41.9 us
    pallas_call x1, Pallas kernels, feed(): pl.pallas_call(feed_kernel, grid=(width // block,), out_shape=(jax.ShapeD...  35.7 us
    unnamed x1, blocking collectives  13.6 us
  transfers between devices with their start and end apart: 10, of which 9 were waited for; matrix products, arithmetic and copies ran while one was open for 10% of the time, Pallas kernels for 6%

profile of v1, /device:TPU:0, one launch (start us, length us, event | category | flops | bytes accessed | tf_op | source)
XLA Modules:
  0.0 590.5 jit_solution(14433523204753738361)
XLA Ops:
  7.2 0.7 all-gather.7.cloned.1.call-update
  8.0 0.7 all-gather.5.cloned.1.call-update
  8.7 1.2 dynamic-slice
  10.6 5.5 concatenate.26
  16.4 13.6 %all-reduce = bf16[9984]{0:T(1024)(128)(2,1)S(1)} all-reduce(bf16[9984]{0:T(1024)(128)(2,1)S(1)} %dynamic-update-slice), channel_id=1, replica_groups=mesh['rep'=8,'shard'=4] {'shard'}, use_global_device_ids=true, to_apply=%add | all-reduce | flops 9984 | bytes 39936
  30.5 0.7 reshape_reshape.9.bq_ref.bk_ref.bv_ref
  31.2 0.8 slice_compare_fusion
  32.7 1.9 multiply_sine_fusion
  34.7 1.7 concatenate.30.ahead_ref
  36.4 1.7 concatenate.31.behind_ref
  38.2 1.0 copy.31.seg_col_ref
  39.3 1.7 concatenate.29.keep_ref
  41.3 0.6 fusion.17
  41.9 0.5 copy-done.3
  42.4 1.6 convert_reduce_fusion.2
  44.0 2.6 fusion.9
  46.6 16.0 %all-gather.5.cloned.1.call-done.wq_ref.wk_ref.wv_ref = bf16[768,2304]{1,0:T(8,128)(2,1)} async-done(((bf16[192,2304]{1,0:T(8,128)(2,1)}), bf16[768,2304]{1,0:T(8,128)(2,1)}) %all-gather.5.cloned.1.call-update) | async-done | bytes 3538960 | tf_op jit(solution)/shard_map/all_gather | solution.py:305
  62.6 67.7 %shard_map.254 = (bf16[1024,768]{1,0:T(8,128)(2,1)}, bf16[1024,2304]{1,0:T(8,128)(2,1)}) custom-call(bf16[1024,768]{1,0:T(8,128)(2,1)} %get-tuple-element.62.a1_ref, bf16[1024,768]{1,0:T(8,128)(2,1)} %get-tuple-element.55.dy_ref, bf16[768,2304]{1,0:T(8,128)(2,1)} %all-gather.5.cloned.1.call-done.wq_ref.wk_ref.wv_ref, ...), custom_call_target="tpu_custom_call" | custom-call | flops 40000000000 | bytes 20000000 | tf_op jit(solution)/shard_map/pallas_call | solution.py:164
  130.3 4.0 convolution_convert_fusion.1
  134.4 7.7 %convolution_convert_fusion = bf16[768,2304]{1,0:T(8,128)(2,1)} fusion(bf16[1024,768]{1,0:T(8,128)(2,1)S(1)} %copy-done.4, bf16[1024,2304]{1,0:T(8,128)(2,1)} %get-tuple-element.35), kind=kOutput, calls=%fused_computation.1 | convolution fusion | flops 3625648128 | bytes 9830400 | tf_op jit(solution)/shard_map/dot_general | solution.py:45
  142.2 0.5 all-gather.9.cloned.1.call-update
  142.8 0.5 all-gather.11.cloned.1.call-update
  143.4 0.6 copy.32
  144.0 16.3 %reduce-scatter.7.cloned.1.call-done = bf16[192,768]{1,0:T(8,128)(2,1)} async-done(((bf16[768,768]{1,0:T(8,128)(2,1)}), bf16[192,768]{1,0:T(8,128)(2,1)}) %reduce-scatter.7.cloned.1.call-update) | async-done | bytes 294928 | tf_op jit(solution)/shard_map/reduce_scatter | solution.py:333
  160.3 43.0 %reduce-scatter.5.cloned.1.call-done = bf16[192,2304]{1,0:T(8,128)(2,1)} async-done(((bf16[768,2304]{1,0:T(8,128)(2,1)}), bf16[192,2304]{1,0:T(8,128)(2,1)}) %reduce-scatter.5.cloned.1.call-update) | async-done | bytes 884752 | tf_op jit(solution)/shard_map/reduce_scatter | solution.py:333
  203.6 38.6 %all-gather.9.cloned.1.call-done.wu_ref = bf16[768,3072]{1,0:T(8,128)(2,1)} async-done(((bf16[192,3072]{1,0:T(8,128)(2,1)}), bf16[768,3072]{1,0:T(8,128)(2,1)}) %all-gather.9.cloned.1.call-update) | async-done | bytes 4718608 | tf_op jit(solution)/shard_map/all_gather | solution.py:305
  242.2 38.9 %all-gather.11.cloned.1.call-done.wd_ref = bf16[3072,768]{1,0:T(8,128)(2,1)} async-done(((bf16[768,768]{1,0:T(8,128)(2,1)}), bf16[3072,768]{1,0:T(8,128)(2,1)}) %all-gather.11.cloned.1.call-update) | async-done | bytes 4718608 | tf_op jit(solution)/shard_map/all_gather | solution.py:305
  281.1 35.7 %shard_map.255 = (f32[1024,768]{1,0:T(8,128)}, f32[1024,768]{1,0:T(8,128)}, bf16[768,3072]{1,0:T(8,128)(2,1)}, bf16[3072,768]{1,0:T(8,128)(2,1)}, f32[1,3072]{1,0:T(1,128)}) custom-call(bf16[1024,768]{1,0:T(8,128)(2,1)} %get-tuple-element.63.a2_ref, bf16[1024,768]{1,0:T(8,128)(2,1)} %get-tuple-element.55.dy_ref, ...), custom_call_target="tpu_custom_call" | custom-call | flops 28999999488 | bytes 30000000 | tf_op jit(solution)/shard_map/pallas_call | solution.py:251
  316.8 48.2 %all-reduce.8.cloned.1.call-done = (bf16[192,2304]{1,0:T(8,128)(2,1)}, bf16[192,768]{1,0:T(8,128)(2,1)}) async-done(((bf16[192,2304]{1,0:T(8,128)(2,1)}, bf16[192,768]{1,0:T(8,128)(2,1)}), (bf16[192,2304]{1,0:T(8,128)(2,1)}, bf16[192,768]{1,0:T(8,128)(2,1)})) %all-reduce.8.cloned.1.call-update) | async-done | bytes 1179664 | tf_op jit(solution)/shard_map/psum | solution.py:334
  365.0 0.7 reduce-scatter.11.cloned.1.call-update
  366.0 3.0 convert_reduce_fusion
  369.1 45.7 %reduce-scatter.9.cloned.1.call-done = bf16[192,3072]{1,0:T(8,128)(2,1)} async-done(((bf16[768,3072]{1,0:T(8,128)(2,1)}), bf16[192,3072]{1,0:T(8,128)(2,1)}) %reduce-scatter.9.cloned.1.call-update) | async-done | bytes 1179664 | tf_op jit(solution)/shard_map/reduce_scatter | solution.py:333
  414.8 50.4 %reduce-scatter.11.cloned.1.call-done = bf16[768,768]{1,0:T(8,128)(2,1)} async-done(((bf16[3072,768]{1,0:T(8,128)(2,1)}), bf16[768,768]{1,0:T(8,128)(2,1)}) %reduce-scatter.11.cloned.1.call-update) | async-done | bytes 1179664 | tf_op jit(solution)/shard_map/reduce_scatter | solution.py:333
  465.2 10.7 %fusion.22 = (f32[768]{0:T(1024)S(1)}, f32[768]{0:T(1024)S(1)}, f32[1024]{0:T(1024)S(1)}, f32[1024]{0:T(1024)S(1)}, f32[1024,768]{1,0:T(8,128)}, /*index=5*/f32[768]{0:T(1024)S(1)}, f32[768]{0:T(1024)S(1)}) fusion(f32[1024,768]{1,0:T(8,128)} %get-tuple-element.36, f32[1024]{0:T(1024)S(1)} %add_rsqrt_fusion, f32[1024]{0:T(1024)S(1)} %broadcast_multiply_fusion.2, ...), kind=kOutput, calls=%fused_computation.49 | convolution fusion | flops 3635670016 | bytes 16156672 | tf_op jit(solution)/shard_map/dot_general | solution.py:49
  476.3 0.5 broadcast.91
  476.8 0.7 reduce.9
  477.6 41.9 %psum.35 = f32[4,2496]{1,0:T(4,128)S(1)} all-reduce(f32[4,2496]{1,0:T(4,128)S(1)} %concatenate.32), channel_id=1, replica_groups=mesh['rep'=8,'shard'=4] {'rep','shard'}, use_global_device_ids=true, to_apply=%region_12.13 | all-reduce | flops 9984 | bytes 79872 | tf_op jit(solution)/shard_map/psum | solution.py:362
  519.5 0.7 dynamic-slice_reduce_fusion.1
  520.2 0.7 dynamic-slice_reduce_fusion
  520.9 0.7 fusion.25
  521.6 4.0 convert_add_fusion.1
  525.6 0.8 copy-done.12
  526.4 2.7 fusion.19
  529.1 1.3 convert_element_type.60
  530.5 0.9 convert_element_type.61
  531.3 47.8 %all-reduce.6.cloned.1.call-done = (bf16[192,3072]{1,0:T(8,128)(2,1)}, bf16[768,768]{1,0:T(8,128)(2,1)}) async-done(((bf16[192,3072]{1,0:T(8,128)(2,1)}, bf16[768,768]{1,0:T(8,128)(2,1)}), (bf16[192,3072]{1,0:T(8,128)(2,1)}, bf16[768,768]{1,0:T(8,128)(2,1)})) %all-reduce.6.cloned.1.call-update) | async-done | bytes 2359312 | tf_op jit(solution)/shard_map/psum | solution.py:338
  579.1 3.0 convert_element_type.62
  582.1 1.6 convert_element_type.63
  (75 shorter events, 3.4 us)
Async XLA Ops:
  7.2 39.4 %all-gather.7.cloned.1.call-start = ((), (), s32[]{:S(2)}) async-start(), calls=%async_computation.5 | async-start | bytes 1474560 | tf_op jit(solution)/shard_map/all_gather | solution.py:305
  7.9 54.7 %all-gather.5.cloned.1.call-start = ((), (), s32[]{:S(2)}) async-start(), calls=%async_computation.4 | async-start | bytes 4423680 | tf_op jit(solution)/shard_map/all_gather | solution.py:305
  8.7 151.6 %reduce-scatter.7.cloned.1.call-start = ((), (), s32[]{:S(2)}) async-start(), calls=%async_computation.9 | async-start | bytes 1474560 | tf_op jit(solution)/shard_map/reduce_scatter | solution.py:333
  34.7 3.5 copy-start.8
  38.2 2.8 copy-start
  41.0 1.4 copy-start.3
  62.6 67.7 %copy-start.1 = (bf16[1024,768]{1,0:T(8,128)(2,1)S(1)}, bf16[1024,768]{1,0:T(8,128)(2,1)}, u32[]{:S(2)}) copy-start(bf16[1024,768]{1,0:T(8,128)(2,1)} %get-tuple-element.55.dy_ref) | copy-start | bytes 4718596
  130.3 4.1 copy-start.4
  134.4 68.9 %reduce-scatter.5.cloned.1.call-start = ((), (), s32[]{:S(2)}) async-start(), calls=%async_computation.8 | async-start | bytes 4423680 | tf_op jit(solution)/shard_map/reduce_scatter | solution.py:333
  142.1 100.1 %all-gather.9.cloned.1.call-start = ((), (), s32[]{:S(2)}) async-start(), calls=%async_computation.6 | async-start | bytes 5898240 | tf_op jit(solution)/shard_map/all_gather | solution.py:305
  142.7 138.4 %all-gather.11.cloned.1.call-start = ((), (), s32[]{:S(2)}) async-start(), calls=%async_computation.7 | async-start | bytes 5898240 | tf_op jit(solution)/shard_map/all_gather | solution.py:305
  143.3 221.7 %all-reduce.8.cloned.1.call-start = ((), (), s32[]{:S(2)}) async-start(), calls=%async_computation.13 | async-start | bytes 2359296 | tf_op jit(solution)/shard_map/psum | solution.py:334
  203.3 211.5 %reduce-scatter.9.cloned.1.call-start = ((), (), s32[]{:S(2)}) async-start(), calls=%async_computation.10 | async-start | bytes 5898240 | tf_op jit(solution)/shard_map/reduce_scatter | solution.py:333
  365.0 100.2 %reduce-scatter.11.cloned.1.call-start = ((), (), s32[]{:S(2)}) async-start(), calls=%async_computation.11 | async-start | bytes 5898240 | tf_op jit(solution)/shard_map/reduce_scatter | solution.py:333
  365.7 213.4 %all-reduce.6.cloned.1.call-start = ((), (), s32[]{:S(2)}) async-start(), calls=%async_computation.12 | async-start | bytes 4718592 | tf_op jit(solution)/shard_map/psum | solution.py:338
  465.2 11.6 %copy-start.9 = (f32[1,3072]{1,0:T(1,128)S(1)}, f32[1,3072]{1,0:T(1,128)}, u32[]{:S(2)}) copy-start(f32[1,3072]{1,0:T(1,128)} %get-tuple-element.37) | copy-start | bytes 36868
  465.2 56.3 %copy-start.2 = (bf16[1024,768]{1,0:T(8,128)(2,1)S(1)}, bf16[1024,768]{1,0:T(8,128)(2,1)}, u32[]{:S(2)}) copy-start(bf16[1024,768]{1,0:T(8,128)(2,1)} %get-tuple-element.55.dy_ref) | copy-start | bytes 4718596
  521.6 4.0 copy-start.10
  521.6 4.0 copy-start.11
  521.6 4.8 copy-start.12
  526.4 2.7 copy-start.6
  526.4 4.0 copy-start.7
  579.1 3.0 copy-start.5
Sparse Core Ops, SparseCore 0:
  9.6 20.5 all-gather.6
  31.8 30.7 all-gather.4
  134.5 25.7 reduce-scatter.6
  162.9 40.4 reduce-scatter.4
  204.7 37.4 all-gather.8
  243.6 37.4 all-gather.10
  284.6 80.2 all-reduce.7
  367.7 47.1 reduce-scatter.8
  417.3 47.8 reduce-scatter.10
  469.1 109.9 all-reduce.5

commit v2 on v1

--- a/solution.py
+++ b/solution.py
@@ -155,7 +155,7 @@
         dqkv_ref[:, pl.ds(spot, PAIR)] = item.astype(BF16)
 
 
-def attention(a1, dy, w_qkv, b_qkv, w_out, tables, segments):
+def attention(a1, dy, w_attn, b_qkv, tables, segments):
     length = a1.shape[0]
     whole = lambda shape: pl.BlockSpec(shape, lambda j: (0, 0))
     column = lambda shift: pl.BlockSpec((D, PAIR), lambda j: (0, shift + j))
@@ -177,7 +177,7 @@
             bias(0),
             bias(PAIRS),
             bias(2 * PAIRS),
-            pl.BlockSpec((PAIR, D), lambda j: (j, 0)),
+            pl.BlockSpec((PAIR, D), lambda j: (j, 3)),
             whole((length, PAIR)),
             whole((length, PAIR)),
             whole((length, PAIR)),
@@ -202,22 +202,26 @@
     )(
         a1,
         dy,
-        w_qkv,
-        w_qkv,
-        w_qkv,
+        w_attn,
+        w_attn,
+        w_attn,
         b_row,
         b_row,
         b_row,
-        w_out,
+        w_attn,
         *tables,
         segments.reshape(length, 1),
         segments.reshape(1, length),
     )
 
 
-def feed_kernel(a2_ref, dy_ref, wu_ref, bu_ref, wd_ref, mlp_ref, da2_ref, gu_ref, gd_ref, gb_ref, h_ref, du_ref):
+def feed_kernel(
+    a2_ref, dy_ref, wu_ref, bu_ref, wd_ref, mlp_ref, da2_ref, grad_ref, gb_ref, h_ref, du_ref
+):
     number = pl.program_id(0)
     length = a2_ref.shape[0]
+    group, owned, block = wu_ref.shape
+    parts = block // wd_ref.shape[1]
     step = length // 4
 
     @pl.when(number == 0)
@@ -225,51 +229,61 @@
         mlp_ref[...] = jnp.zeros_like(mlp_ref)
         da2_ref[...] = jnp.zeros_like(da2_ref)
 
+    wu = wu_ref[...].reshape(D, block)
+    wd = wd_ref[...].reshape(block, D)
     total = None
     for lo in range(0, length, step):
         rows = slice(lo, lo + step)
-        u = dot(a2_ref[rows, :], wu_ref[...]) + bu_ref[...]
+        u = dot(a2_ref[rows, :], wu) + bu_ref[...]
         area = 0.5 + 0.5 * lax.erf(u * (0.5**0.5))
         h_ref[rows, :] = (u * area).astype(BF16)
         slope = area + u * (jnp.exp(u * u * -0.5) * 0.3989422804014327)
-        du = (across(dy_ref[rows, :], wd_ref[...]) * slope).astype(BF16)
+        du = (across(dy_ref[rows, :], wd) * slope).astype(BF16)
         du_ref[rows, :] = du
         part = jnp.sum(du.astype(F32), 0, keepdims=True)
         total = part if total is None else total + part
-        mlp_ref[rows, :] += dot(h_ref[rows, :], wd_ref[...])
-        da2_ref[rows, :] += across(du, wu_ref[...])
+        mlp_ref[rows, :] += dot(h_ref[rows, :], wd)
+        da2_ref[rows, :] += across(du, wu)
     gb_ref[...] = total
-    gu_ref[...] = contract_rows(a2_ref[...], du_ref[...]).astype(gu_ref.dtype)
-    gd_ref[...] = contract_rows(h_ref[...], dy_ref[...]).astype(gd_ref.dtype)
-
-
-def feed(a2, dy, w_up, b_up, w_down):
+    gu = contract_rows(a2_ref[...], du_ref[...]).astype(BF16)
+    spot = pl.multiple_of(number * owned, owned)
+    grad_ref[:, pl.ds(spot, owned), :] = gu.reshape(group, owned, block)
+    gd = contract_rows(h_ref[...], dy_ref[...]).astype(BF16)
+    held = wd_ref.shape[1]
+    lead = grad_ref.shape[1] - held
+    grad_ref[pl.ds(number * parts, parts), lead:, :] = gd.reshape(parts, held, D)
+
+
+def feed(a2, dy, w_feed, b_up):
     length = a2.shape[0]
-    width = w_up.shape[1]
-    block = 512
+    group = w_feed.shape[0]
+    owned = D // group
+    width = b_up.shape[0]
+    held = width // group
+    block = D
+    parts = block // held
+    chunks = width // block
     whole = lambda shape: pl.BlockSpec(shape, lambda j: (0, 0))
     return pl.pallas_call(
         feed_kernel,
-        grid=(width // block,),
+        grid=(chunks,),
         out_shape=(
             jax.ShapeDtypeStruct((length, D), F32),
             jax.ShapeDtypeStruct((length, D), F32),
-            jax.ShapeDtypeStruct((D, width), BF16),
-            jax.ShapeDtypeStruct((width, D), BF16),
+            jax.ShapeDtypeStruct(w_feed.shape, BF16),
             jax.ShapeDtypeStruct((1, width), F32),
         ),
         in_specs=[
             whole((length, D)),
             whole((length, D)),
-            pl.BlockSpec((D, block), lambda j: (0, j)),
+            pl.BlockSpec((group, owned, block), lambda j: (0, j, 0)),
             pl.BlockSpec((1, block), lambda j: (0, j)),
-            pl.BlockSpec((block, D), lambda j: (j, 0)),
+            pl.BlockSpec((parts, held, D), lambda j: (j, chunks * owned // held, 0)),
         ],
         out_specs=(
             whole((length, D)),
             whole((length, D)),
-            pl.BlockSpec((D, block), lambda j: (0, j)),
-            pl.BlockSpec((block, D), lambda j: (j, 0)),
+            pl.BlockSpec(w_feed.shape, lambda j: (0, 0, 0)),
             pl.BlockSpec((1, block), lambda j: (0, j)),
         ),
         scratch_shapes=[
@@ -282,7 +296,16 @@
         cost_estimate=pl.CostEstimate(
             flops=29_000_000_000, bytes_accessed=30_000_000, transcendentals=6_000_000
         ),
-    )(a2, dy, w_up, b_up.reshape(1, width), w_down)
+    )(a2, dy, w_feed, b_up.reshape(1, width), w_feed)
+
+
+def scatter_owner(grad):
+    flat = grad.reshape(-1, grad.shape[-1])
+    return lax.psum_scatter(flat, "shard", scatter_dimension=0, tiled=True)
+
+
+def sum_copies(grads):
+    return lax.psum(grads, "rep")
 
 
 def local(
@@ -311,13 +334,14 @@
     gain_one, bias_one, gain_two, bias_two, b_qkv, b_out, b_up, b_down = tuple(
         packed[:, offset : offset + size].reshape(-1) for offset, size in zip(offsets, sizes)
     )
-    w_out = gather(out_weight)
-    w_qkv = gather(qkv_weight)
-    up_weight, down_weight, w_qkv, w_out = lax.optimization_barrier(
-        (up_weight, down_weight, w_qkv, w_out)
-    )
-    w_up = gather(up_weight)
-    w_down = gather(down_weight)
+    owned, width = up_weight.shape
+    chunks = width // D
+    w_attn = gather(jnp.concatenate([qkv_weight, out_weight], 1))
+    stacked = jnp.concatenate(
+        [up_weight[:, index * D : (index + 1) * D] for index in range(chunks)] + [down_weight], 0
+    )
+    stacked, w_attn = lax.optimization_barrier((stacked, w_attn))
+    w_feed = lax.all_gather(stacked, "shard", axis=0, tiled=False)
 
     x = hidden_in.astype(F32)
     center = x - jnp.mean(x, -1, keepdims=True)
@@ -329,14 +353,19 @@
     dy_float = dy.astype(F32)
     tables = turn_tables(positions(segment_ids))
 
-    o, dqkv = attention(a1, dy, w_qkv, b_qkv, w_out, tables, segment_ids)
-    scatter = lambda item: lax.psum_scatter(item, "shard", scatter_dimension=0, tiled=True)
-    g_qkv = lax.psum(scatter(contract_rows(a1, dqkv).astype(BF16)), "rep")
-    g_out = lax.psum(scatter(contract_rows(o, dy).astype(BF16)), "rep")
-    mlp, da2, g_up, g_down, g_up_bias = feed(a2, dy, w_up, b_up, w_down)
-    g_up, g_down, g_qkv, g_out = lax.optimization_barrier((g_up, g_down, g_qkv, g_out))
-    g_up = lax.psum(scatter(g_up), "rep")
-    g_down = lax.psum(scatter(g_down), "rep")
+    o, dqkv = attention(a1, dy, w_attn, b_qkv, tables, segment_ids)
+    g_attn = jnp.concatenate([contract_rows(a1, dqkv), contract_rows(o, dy)], 1).astype(BF16)
+    g_attn, w_feed = lax.optimization_barrier((g_attn, w_feed))
+    g_attn = scatter_owner(g_attn.reshape(group, owned, -1))
+    mlp, da2, g_feed, g_up_bias = feed(a2, dy, w_feed, b_up)
+    g_feed, g_attn = lax.optimization_barrier((g_feed, g_attn))
+    g_feed = scatter_owner(g_feed)
+    g_attn, g_feed = sum_copies((g_attn, g_feed))
+    w_qkv, w_out = w_attn[:, : 3 * D], w_attn[:, 3 * D :]
+    lead = chunks * owned
+    g_up = jnp.concatenate(
+        [g_feed[index * owned : (index + 1) * owned] for index in range(chunks)], 1
+    )
 
     da1 = across(dqkv, w_qkv)
     mixed = (x + (dot(o, w_out) + b_out) + (mlp + b_down)).astype(BF16)
@@ -369,13 +398,13 @@
         own[1],
         own[2],
         own[3],
-        g_qkv.astype(F32),
+        g_attn[:, : 3 * D].astype(F32),
         own[4],
-        g_out.astype(F32),
+        g_attn[:, 3 * D :].astype(F32),
         own[5],
         g_up.astype(F32),
         own[6],
-        g_down.astype(F32),
+        g_feed[lead:].astype(F32),
         own[7],
     )
 

time: 591 us -> 446 us (0.75)
  waiting for transfers between devices: 348 us -> 203 us
    reduce_scatter x4 -> x2, waiting for transfers between devices: 155 us -> 91.2 us  [scatter_owner(): return lax.psum_scatter(flat, 'shard', scatter_dimension=0, tiled=True)]
    all_gather x4 -> x1, waiting for transfers between devices: 93.5 us -> 36.4 us  [local(): gather = lambda item: lax.all_gather(item, 'shard', axis=0, tiled=True)]
    psum x2 -> x1, waiting for transfers between devices: 96 us -> 75.1 us  [sum_copies(): return lax.psum(grads, 'rep')]
  transfers between devices with their start and end apart: 10 -> 5, of which waited for: 9 -> 4; matrix products, arithmetic and copies ran while one was open for 10% -> 13% of each run, Pallas kernels for 6% -> 24%
where the time goes in v2:
time: 446 us
  waiting for transfers between devices  203 us (46%)
  Pallas kernels  106 us (24%)
  blocking collectives  54.3 us (12%)
  other arithmetic  28.2 us (6%)
  matrix products  22.2 us (5%)
  local copies, waits for them, and re-layouts  17.6 us (4%)
  between operations  14.8 us (3%)
    reduce_scatter x2, waiting for transfers between devices, scatter_owner(): return lax.psum_scatter(flat, 'shard', scatter_dimension=0, tiled=True)  91.2 us
    psum x1, waiting for transfers between devices, sum_copies(): return lax.psum(grads, 'rep')  75.1 us
    pallas_call x1, Pallas kernels, attention(): pl.pallas_call(functools.partial(attention_kernel, 256), grid=(PAIRS,), o...  67.9 us
    psum x1, blocking collectives, local(): small = lax.psum(small, ('rep', 'shard')).reshape(group, -1)  43.9 us
    pallas_call x1, Pallas kernels, feed(): pl.pallas_call(feed_kernel, grid=(chunks,), out_shape=(jax.ShapeDtypeStru...  37.9 us
    all_gather x1, waiting for transfers between devices, local(): gather = lambda item: lax.all_gather(item, 'shard', axis=0, tiled=True)  36.4 us
    dot_general x1, matrix products, across(): lax.dot_general(left, right, (((1,), (1,)), ((), ())), preferred_element_...  10.8 us
    unnamed x1, blocking collectives  10.3 us
  transfers between devices with their start and end apart: 5, of which 4 were waited for; matrix products, arithmetic and copies ran while one was open for 13% of the time, Pallas kernels for 24%

profile of v2, /device:TPU:0, one launch (start us, length us, event | category | flops | bytes accessed | tf_op | source)
XLA Modules:
  0.0 446.0 jit_solution(12253336526657368341)
XLA Ops:
  7.2 2.5 pad_maximum_fusion.1
  9.8 0.7 slice_dynamic-update-slice_fusion.3
  10.5 0.7 slice_dynamic-update-slice_fusion.2
  11.3 0.7 slice_dynamic-update-slice_fusion.1
  12.0 0.7 slice_dynamic-update-slice_fusion
  12.9 1.1 constant_dynamic-update-slice_fusion
  14.0 36.4 %all-gather.4.cloned.1.call-done.wq_ref.wk_ref.wv_ref.wo_ref = bf16[768,3072]{1,0:T(8,128)(2,1)} async-done(((bf16[192,3072]{1,0:T(8,128)(2,1)}), bf16[768,3072]{1,0:T(8,128)(2,1)}) %all-gather.4.cloned.1.call-update) | async-done | bytes 4718608 | tf_op jit(solution)/shard_map/all_gather | solution.py:328
  50.6 0.3 reduce-window.9
  51.0 0.6 dynamic-slice
  52.4 0.3 dynamic-update-slice
  52.7 10.3 %all-reduce = bf16[9984]{0:T(1024)(128)(2,1)S(1)} all-reduce(bf16[9984]{0:T(1024)(128)(2,1)S(1)} %dynamic-update-slice), channel_id=1, replica_groups=mesh['rep'=8,'shard'=4] {'shard'}, use_global_device_ids=true, to_apply=%add | all-reduce | flops 9984 | bytes 39936
  63.2 0.7 reshape_reshape.9.bq_ref.bk_ref.bv_ref
  64.2 1.0 copy.33.seg_col_ref
  65.3 0.1 slice_reduce_fusion
  65.5 1.9 multiply_sine_fusion
  67.5 1.7 concatenate.46.behind_ref
  69.2 1.7 concatenate.45.ahead_ref
  71.0 1.7 concatenate.44.keep_ref
  72.8 0.3 convert_reduce_fusion.1
  73.1 0.6 fusion.19
  73.7 0.5 copy-done.5
  74.2 1.6 convert_reduce_fusion.2
  75.7 2.6 fusion.11
  78.3 67.9 %shard_map.254 = (bf16[1024,768]{1,0:T(8,128)(2,1)}, bf16[1024,2304]{1,0:T(8,128)(2,1)}) custom-call(bf16[1024,768]{1,0:T(8,128)(2,1)} %get-tuple-element.58.a1_ref, bf16[1024,768]{1,0:T(8,128)(2,1)} %get-tuple-element.47.dy_ref, bf16[768,3072]{1,0:T(8,128)(2,1)} %all-gather.4.cloned.1.call-done.wq_ref.wk_ref.wv_ref.wo_ref, ...), custom_call_target="tpu_custom_call" | custom-call | flops 40000000000 | bytes 20000000 | tf_op jit(solution)/shard_map/pallas_call | solution.py:164
  146.2 3.0 convolution_convert_fusion.1
  149.2 0.3 copy-done.6
  149.5 4.4 convolution_convert_fusion
  153.9 2.8 pad_maximum_fusion
  156.8 0.6 copy.36
  157.4 37.9 %shard_map.255 = (f32[1024,768]{1,0:T(8,128)}, f32[1024,768]{1,0:T(8,128)}, bf16[4,1536,768]{2,1,0:T(8,128)(2,1)}, f32[1,3072]{1,0:T(1,128)}) custom-call(bf16[1024,768]{1,0:T(8,128)(2,1)} %get-tuple-element.59.a2_ref, bf16[1024,768]{1,0:T(8,128)(2,1)} %get-tuple-element.47.dy_ref, bf16[4,1536,768]{2,1,0:T(8,128)(2,1)} %bitcast.39, f32[1,3072]{1,0:T(1,128)} %bitcast.32, ...), custom_call_target="tpu_custom_call" | custom-call | flops 28999999488 | bytes 30000000 | tf_op jit(solution)/shard_map/pallas_call | solution.py:267
  195.3 10.5 %reduce-scatter.3.cloned.1.call-done = bf16[192,3072]{1,0:T(8,128)(2,1)} async-done(((bf16[768,3072]{1,0:T(8,128)(2,1)}), bf16[192,3072]{1,0:T(8,128)(2,1)}) %reduce-scatter.3.cloned.1.call-update) | async-done | bytes 1179664 | tf_op jit(solution)/shard_map/reduce_scatter | solution.py:304
  205.8 0.3 all-reduce.4.cloned.1.call-start
  206.1 80.8 %reduce-scatter.5.cloned.1.call-done = bf16[1536,768]{1,0:T(8,128)(2,1)} async-done(((bf16[6144,768]{1,0:T(8,128)(2,1)}), bf16[1536,768]{1,0:T(8,128)(2,1)}) %reduce-scatter.5.cloned.1.call-update) | async-done | bytes 2359312 | tf_op jit(solution)/shard_map/reduce_scatter | solution.py:304
  287.2 3.0 convert_reduce_fusion
  290.3 10.8 %fusion.25 = (f32[768]{0:T(1024)S(1)}, f32[768]{0:T(1024)S(1)}, f32[1024]{0:T(1024)S(1)}, f32[1024]{0:T(1024)S(1)}, f32[1024,768]{1,0:T(8,128)}, /*index=5*/f32[768]{0:T(1024)S(1)}, f32[768]{0:T(1024)S(1)}) fusion(f32[1024,768]{1,0:T(8,128)} %get-tuple-element.32, f32[1024]{0:T(1024)S(1)} %add_rsqrt_fusion, f32[1024]{0:T(1024)S(1)} %broadcast_multiply_fusion.2, ...), kind=kOutput, calls=%fused_computation.63 | convolution fusion | flops 3635670016 | bytes 16156672 | tf_op jit(solution)/shard_map/dot_general | solution.py:49
  301.4 0.5 broadcast.91
  301.9 0.7 reduce.9
  302.7 43.9 %psum.21 = f32[4,2496]{1,0:T(4,128)S(1)} all-reduce(f32[4,2496]{1,0:T(4,128)S(1)} %concatenate.48), channel_id=1, replica_groups=mesh['rep'=8,'shard'=4] {'rep','shard'}, use_global_device_ids=true, to_apply=%region_12.13 | all-reduce | flops 9984 | bytes 79872 | tf_op jit(solution)/shard_map/psum | solution.py:391
  346.6 0.7 dynamic-slice_reduce_fusion.1
  347.3 0.7 dynamic-slice_reduce_fusion
  348.0 0.7 fusion.29
  348.6 4.0 convert_add_fusion.1
  352.6 4.0 fusion.21
  356.6 75.1 %all-reduce.4.cloned.1.call-done = (bf16[192,3072]{1,0:T(8,128)(2,1)}, bf16[1536,768]{1,0:T(8,128)(2,1)}) async-done(((bf16[192,3072]{1,0:T(8,128)(2,1)}, bf16[1536,768]{1,0:T(8,128)(2,1)}), (bf16[192,3072]{1,0:T(8,128)(2,1)}, bf16[1536,768]{1,0:T(8,128)(2,1)})) %all-reduce.4.cloned.1.call-update) | async-done | bytes 3538960 | tf_op jit(solution)/shard_map/psum | solution.py:308
  431.7 2.0 slice_convert_fusion.2
  433.7 2.5 slice_convert_fusion.1
  436.2 1.6 slice_convert_fusion
  437.8 1.7 maximum_convert_fusion
  (86 shorter events, 2.2 us)
Async XLA Ops:
  7.2 2.6 copy-start.7
  7.2 43.2 %all-gather.4.cloned.1.call-start = ((), (), s32[]{:S(2)}) async-start(), calls=%async_computation.2 | async-start | bytes 5898240 | tf_op jit(solution)/shard_map/all_gather | solution.py:328
  9.7 3.0 copy-start.8
  9.7 147.0 %all-gather.6.cloned.1.call-start = ((), (), s32[]{:S(2)}) async-start(), calls=%async_computation.5 | async-start | bytes 11796480 | tf_op jit(solution)/shard_map/all_gather | solution.py:344
  12.8 37.7 %copy-start.9 = (s32[1024]{0:T(1024)S(1)}, s32[1024]{0:T(1024)}, u32[]{:S(2)}) copy-start(s32[1024]{0:T(1024)} %param.16) | copy-start | bytes 12292
  12.8 38.2 %copy-start.19 = (u32[32]{0:T(128)S(1)}, u32[32]{0:T(128)}, u32[]{:S(2)}) copy-start(u32[32]{0:T(128)} %constant.43) | copy-start | bytes 388
  12.8 39.5 %copy-start.11 = (bf16[576]{0:T(1024)(128)(2,1)S(1)}, bf16[576]{0:T(1024)(128)(2,1)}, u32[]{:S(2)}) copy-start(bf16[576]{0:T(1024)(128)(2,1)} %param.23) | copy-start | bytes 3460
  12.8 39.5 %copy-start.12 = (bf16[768]{0:T(1024)(128)(2,1)S(1)}, bf16[768]{0:T(1024)(128)(2,1)}, u32[]{:S(2)}) copy-start(bf16[768]{0:T(1024)(128)(2,1)} %param.27) | copy-start | bytes 4612
  12.8 39.5 %copy-start.13 = (bf16[192]{0:T(256)(128)(2,1)S(1)}, bf16[192]{0:T(256)(128)(2,1)}, u32[]{:S(2)}) copy-start(bf16[192]{0:T(256)(128)(2,1)} %param.18) | copy-start | bytes 1156
  12.8 39.5 %copy-start.14 = (bf16[192]{0:T(256)(128)(2,1)S(1)}, bf16[192]{0:T(256)(128)(2,1)}, u32[]{:S(2)}) copy-start(bf16[192]{0:T(256)(128)(2,1)} %param.19) | copy-start | bytes 1156
  12.8 39.5 %copy-start.15 = (bf16[192]{0:T(256)(128)(2,1)S(1)}, bf16[192]{0:T(256)(128)(2,1)}, u32[]{:S(2)}) copy-start(bf16[192]{0:T(256)(128)(2,1)} %param.20) | copy-start | bytes 1156
  12.8 39.5 %copy-start.16 = (bf16[192]{0:T(256)(128)(2,1)S(1)}, bf16[192]{0:T(256)(128)(2,1)}, u32[]{:S(2)}) copy-start(bf16[192]{0:T(256)(128)(2,1)} %param.21) | copy-start | bytes 1156
  12.8 39.5 %copy-start.17 = (bf16[192]{0:T(256)(128)(2,1)S(1)}, bf16[192]{0:T(256)(128)(2,1)}, u32[]{:S(2)}) copy-start(bf16[192]{0:T(256)(128)(2,1)} %param.25) | copy-start | bytes 1156
  12.8 39.5 %copy-start.18 = (bf16[192]{0:T(256)(128)(2,1)S(1)}, bf16[192]{0:T(256)(128)(2,1)}, u32[]{:S(2)}) copy-start(bf16[192]{0:T(256)(128)(2,1)} %param.29) | copy-start | bytes 1156
  50.4 155.4 %reduce-scatter.3.cloned.1.call-start = ((), (), s32[]{:S(2)}) async-start(), calls=%async_computation.3 | async-start | bytes 5898240 | tf_op jit(solution)/shard_map/reduce_scatter | solution.py:304
  71.0 1.8 copy-start
  72.8 1.4 copy-start.5
  78.3 67.9 %copy-start.1 = (bf16[1024,768]{1,0:T(8,128)(2,1)S(1)}, bf16[1024,768]{1,0:T(8,128)(2,1)}, u32[]{:S(2)}) copy-start(bf16[1024,768]{1,0:T(8,128)(2,1)} %get-tuple-element.47.dy_ref) | copy-start | bytes 4718596
  146.2 3.0 copy-start.3
  146.2 3.3 copy-start.6
  156.8 130.1 %reduce-scatter.5.cloned.1.call-start = ((), (), s32[]{:S(2)}) async-start(), calls=%async_computation.4 | async-start | bytes 11796480 | tf_op jit(solution)/shard_map/reduce_scatter | solution.py:304
  205.8 225.9 %all-reduce.4.cloned.1.call-start = ((), (), s32[]{:S(2)}) async-start(), calls=%async_computation.6 | async-start | bytes 7077888 | tf_op jit(solution)/shard_map/psum | solution.py:308
  290.3 11.6 %copy-start.10 = (f32[1,3072]{1,0:T(1,128)S(1)}, f32[1,3072]{1,0:T(1,128)}, u32[]{:S(2)}) copy-start(f32[1,3072]{1,0:T(1,128)} %get-tuple-element.33) | copy-start | bytes 36868
  290.3 58.3 %copy-start.2 = (bf16[1024,768]{1,0:T(8,128)(2,1)S(1)}, bf16[1024,768]{1,0:T(8,128)(2,1)}, u32[]{:S(2)}) copy-start(bf16[1024,768]{1,0:T(8,128)(2,1)} %get-tuple-element.47.dy_ref) | copy-start | bytes 4718596
  348.6 4.0 copy-start.20
  348.6 4.0 copy-start.21
  431.7 4.5 copy-start.4
Sparse Core Ops, SparseCore 0:
  10.2 40.1 all-gather.3
  52.5 64.2 all-gather.5
  156.9 48.8 reduce-scatter.2
  208.4 78.4 reduce-scatter.4
  290.9 140.7 all-reduce.3
